TPU v7x, 256 devices: a whole 4x4x8 slice. The times are simulated.
256 devices in a mesh: dp: 8 (over x, y_lo), expert: 32 (over z, y_hi, core).
Axes of the slice: x: 4, y: 4 (y_hi: 2, y_lo: 2; y = y_hi * 2 + y_lo), z: 8, core: 2. Of those that a mesh axis runs over, the one named last changes fastest.
Arguments:
- tokens: bfloat16 [32768, 2048], P(('dp', 'expert')), may hold values from -6 to 6
- routes: int32 [32768, 2], P(('dp', 'expert')), may hold values from 0 to 31, all different within a row; in each aligned block of 128 rows (0 to 127, 128 to 255, ...) at most 16 rows name the same one
- gate_probs: bfloat16 [32768, 2], P(('dp', 'expert')), may hold values from 0.049804688 to 1
- cotangent: bfloat16 [32768, 2048], P(('dp', 'expert')), may hold values from -6 to 6
- expert_weights: bfloat16 [32, 2048, 2304], P('expert'), may hold values from -0.125 to 0.125
Outputs:
- token_grads: bfloat16 [32768, 2048], P(('dp', 'expert'))
- prob_grads: float32 [32768, 2], P(('dp', 'expert'))
- weight_grads: float32 [32, 2048, 2304], P('expert', 'dp')
Inputs may be any that keep to these rules, and one draw needn't show every extreme that they name: `routes`: each token names 2 different experts and every expert is named by some token. In each aligned block of 128 tokens (the tokens of one device) no expert is named by more than 16 tokens, and in some block one expert is named by exactly 16.
All inputs are finite; a program needn't handle non-finite values.
Results may differ from a plain program's by a relative error of at most 0.017.
Values may be sent and summed in bfloat16 or wider, within the bound.
No kernel may reach another device: no remote copies, remote signals or barrier semaphores. Data moves between devices by JAX's collectives and lax.ppermute only.
A program may use at most 192 MiB of HBM per device.

v0:
```python
import functools

import jax
import jax.numpy as jnp
from jax import lax
from jax.experimental import pallas as pl
from jax.experimental.pallas import tpu as pltpu
from jax.sharding import PartitionSpec as P

BF = jnp.bfloat16
F32 = jnp.float32
I32 = jnp.int32
D = 2048
F = 768
T = 128
CAP = 16
NZ = 8
NQ = 4
FB = 256
NF = F // FB
ROWS = NZ * NQ * CAP
EXTRA = 128
MIB = 1024 * 1024
NT = (((1,), (1,)), ((), ()))
TN = (((0,), (0,)), ((), ()))
ANY = pl.BlockSpec(memory_space=pl.ANY)
together = lax.optimization_barrier


def z_shift(value, step):
    return lax.ppermute(value, "expert", [(i, (i + NQ * step) % 32) for i in range(32)])


def plane_swap(value, mask):
    return lax.ppermute(value, "expert", [(i, i ^ mask) for i in range(32)])


def x_shift(value, step):
    return lax.ppermute(value, "dp", [(i, (i + 2 * step) % 8) for i in range(8)])


def y_swap(value):
    return lax.ppermute(value, "dp", [(i, i ^ 1) for i in range(8)])


def params(mib):
    return pltpu.CompilerParams(vmem_limit_bytes=mib * MIB)


def cost(flops, moved):
    return pl.CostEstimate(flops=flops // 1024, bytes_accessed=moved // 1024, transcendentals=0)


def columns(pairs):
    diagonal = lax.broadcasted_iota(I32, (T, T), 0) == lax.broadcasted_iota(I32, (T, T), 1)
    eye = diagonal.astype(F32).astype(BF)
    return lax.dot_general(eye, pairs.astype(F32).astype(BF), NT, preferred_element_type=F32)


def pack_kernel(tokens, cotangent, routes, probs, out):
    out[:, :D] = tokens[...]
    out[:, D : 2 * D] = cotangent[...]
    lane = lax.broadcasted_iota(I32, (T, EXTRA), 1)
    r, p = columns(routes[...]), columns(probs[...])
    meta = jnp.where(lane == 0, r[:, 0:1], jnp.where(lane == 1, r[:, 1:2], 0.0))
    meta += jnp.where(lane == 2, p[:, 0:1], jnp.where(lane == 3, p[:, 1:2], 0.0))
    out[:, 2 * D :] = meta.astype(BF)


def pack(tokens, cotangent, routes, probs):
    return pl.pallas_call(
        pack_kernel,
        out_shape=jax.ShapeDtypeStruct((T, 2 * D + EXTRA), BF),
        cost_estimate=cost(0, 4 * T * D * 2),
        compiler_params=params(8),
    )(tokens, cotangent, routes.T, probs.T)


def slots(r0, r1, expert, place):
    first = (r0 == expert).astype(F32)
    second = (r1 == expert).astype(F32)
    named = first + second
    row = lax.broadcasted_iota(I32, (T, T), 0)
    col = lax.broadcasted_iota(I32, (T, T), 1)
    before = (col < row).astype(F32).astype(BF)
    position = jnp.dot(before, named.astype(BF), preferred_element_type=F32)
    here = (position == place).astype(F32)
    return first * here, second * here


def select_kernel(plan, n, *refs):
    metas, ins, outs, hot = refs[:n], refs[n : 2 * n], refs[2 * n : -1], refs[-1]
    c = pl.program_id(0)

    @pl.when(c == 0)
    def _():
        me = lax.axis_index("expert")
        z, q = me // NQ, me % NQ
        for i, (block, step, _, _) in enumerate(plan):
            lane = lax.broadcasted_iota(I32, (T, NQ * CAP), 1)
            plane = (z + step + NZ) % NZ
            expert = (plane * NQ + jnp.bitwise_xor(q, lane // CAP)).astype(F32)
            place = (lane % CAP).astype(F32)
            meta = metas[block][...].astype(F32)
            one, two = slots(meta[:, 0:1], meta[:, 1:2], expert, place)
            hot[0, i] = (one + two).astype(BF)
            hot[1, i] = (one * meta[:, 2:3] + two * meta[:, 3:4]).astype(BF)

    for i, (block, _, experts, at) in enumerate(plan):
        rows = lax.dot_general(hot[c // 2, i], ins[block][...], TN, preferred_element_type=F32)
        rows = rows.astype(BF)
        for j in experts:
            outs[j][at : at + CAP, :] = rows[j * CAP : (j + 1) * CAP, :]


def select(plan, ins):
    n = len(ins)
    width = 1024
    height = max(at for _, _, _, at in plan) + CAP
    return pl.pallas_call(
        functools.partial(select_kernel, plan, n),
        grid=(2 * D // width,),
        in_specs=[pl.BlockSpec((T, EXTRA), lambda c: (0, 2 * D // EXTRA))] * n
        + [pl.BlockSpec((T, width), lambda c: (0, c))] * n,
        out_specs=[pl.BlockSpec((height, width), lambda c: (0, c))] * NQ,
        out_shape=[jax.ShapeDtypeStruct((height, 2 * D), BF)] * NQ,
        scratch_shapes=[pltpu.VMEM((2, len(plan), T, NQ * CAP), BF)],
        cost_estimate=cost(2 * n * 64 * T * 2 * D, n * 3 * T * D * 2),
        compiler_params=params(10),
    )(*ins, *ins)


def dot_columns(dots):
    lane = lax.broadcasted_iota(I32, dots.shape, 1)
    high = dots.astype(BF).astype(F32)
    return jnp.where(lane == 0, high, jnp.where(lane == 1, dots - high, 0.0)).astype(BF)


def place_rows(order, out_rows, grad_all, sems):
    me = lax.axis_index("expert")
    z, q = me // NQ, me % NQ
    copies = []
    for i, (step, near) in enumerate(order):
        owner = ((z + step + NZ) % NZ) * NQ + jnp.bitwise_xor(q, near)
        copies.append(
            pltpu.make_async_copy(
                out_rows.at[pl.ds(i * CAP, CAP)],
                grad_all.at[pl.ds(pl.multiple_of(owner * CAP, CAP), CAP)],
                sems.at[i],
            )
        )
    for copy in copies:
        copy.start()
    for copy in copies:
        copy.wait()


def expert_kernel(pieces, order, grads, aliased, gate_w, up_w, down_w, *refs):
    ins = refs[: len(pieces)]
    refs = refs[len(pieces) + aliased :]
    if grads:
        xs, fac, grad_all, rows, dot_acc, acc, out_rows, sems = refs
    else:
        xs, fac, dots, rows, dot_acc = refs
    f = pl.program_id(0)

    @pl.when(f == 0)
    def _():
        at = 0
        for size, ref in zip(pieces, ins):
            rows[at : at + size, :] = ref[...]
            at += size
        dot_acc[...] = jnp.zeros_like(dot_acc)
        if grads:
            acc[...] = jnp.zeros_like(acc)

    x = rows[:, :D]
    gate = jnp.dot(x, gate_w[...], preferred_element_type=F32)
    up = jnp.dot(x, up_w[...], preferred_element_type=F32)
    dh = jnp.dot(rows[:, D:], down_w[...], preferred_element_type=F32)
    sig = jax.nn.sigmoid(gate)
    active = gate * sig
    hidden = (active * up).astype(BF)
    d_gate = (dh * up * sig * (1.0 + gate * (1.0 - sig))).astype(BF)
    d_up = (dh * active).astype(BF)
    at = pl.multiple_of(f * FB, FB)
    fac[:, pl.ds(at, FB)] = d_gate
    fac[:, pl.ds(F + at, FB)] = d_up
    fac[:, pl.ds(2 * F + at, FB)] = hidden
    prod = hidden.astype(F32) * dh
    dot_acc[...] += prod[:, :128] + prod[:, 128:]
    if grads:
        acc[...] += lax.dot_general(d_gate, gate_w[...], NT, preferred_element_type=F32)
        acc[...] += lax.dot_general(d_up, up_w[...], NT, preferred_element_type=F32)

    @pl.when(f == NF - 1)
    def _():
        dp = lax.axis_index("dp")
        xi, yi = dp // 2, dp % 2
        for part in range(2):
            for chunk in range(4):
                for half in range(2):
                    source = ((xi + chunk) % 4) * 2 + jnp.bitwise_xor(yi, half)
                    source = pl.multiple_of(part * D + source * 256, 256)
                    to = part * D + (chunk * 2 + half) * 256
                    xs[:, to : to + 256] = rows[:, pl.ds(source, 256)]
        total = jnp.sum(dot_acc[...], axis=1, keepdims=True)
        total = jnp.broadcast_to(total, dot_acc.shape)
        if grads:
            out_rows[:, :D] = acc[...].astype(BF)
            out_rows[:, D:] = dot_columns(total)
            place_rows(order, out_rows, grad_all, sems)
        else:
            dots[...] = total


def expert_pass(weights, pieces, sizes, order, block, held, grads):
    rows = sum(sizes)
    whole = lambda f: (0, 0)
    mine = lambda f: (block, 0)
    outs = [pl.BlockSpec((rows, 2 * D), mine), pl.BlockSpec((rows, 3 * F), mine)]
    shapes = [jax.ShapeDtypeStruct((ROWS, 2 * D), BF), jax.ShapeDtypeStruct((ROWS, 3 * F), BF)]
    scratch = [pltpu.VMEM((rows, 2 * D), BF), pltpu.VMEM((rows, 128), F32)]
    if grads:
        outs.append(ANY)
        shapes.append(jax.ShapeDtypeStruct((ROWS, D + EXTRA), BF))
        scratch += [
            pltpu.VMEM((rows, D), F32),
            pltpu.VMEM((rows, D + EXTRA), BF),
            pltpu.SemaphoreType.DMA((rows // CAP,)),
        ]
    else:
        outs.append(pl.BlockSpec((rows, 128), whole))
        shapes.append(jax.ShapeDtypeStruct((rows, 128), F32))
    return pl.pallas_call(
        functools.partial(expert_kernel, sizes, order, grads, len(held)),
        grid=(NF,),
        in_specs=[
            pl.BlockSpec((D, FB), lambda f: (0, f)),
            pl.BlockSpec((D, FB), lambda f: (0, f + NF)),
            pl.BlockSpec((D, FB), lambda f: (0, f + 2 * NF)),
        ]
        + [pl.BlockSpec((size, 2 * D), whole) for size in sizes]
        + [ANY] * len(held),
        out_specs=outs,
        out_shape=shapes,
        scratch_shapes=scratch,
        input_output_aliases={3 + len(pieces) + i: i for i in range(len(held))},
        cost_estimate=cost(2 * rows * D * (5 if grads else 3) * F, D * 3 * F * 2),
        compiler_params=params(24),
    )(weights, weights, weights, *pieces, *held)


def grad_kernel(order, gate_w, up_w, gate_f, up_f, dots, held, grad_all, acc, out_rows, sems):
    f = pl.program_id(0)

    @pl.when(f == 0)
    def _():
        acc[...] = jnp.zeros_like(acc)

    acc[...] += lax.dot_general(gate_f[...], gate_w[...], NT, preferred_element_type=F32)
    acc[...] += lax.dot_general(up_f[...], up_w[...], NT, preferred_element_type=F32)

    @pl.when(f == NF - 1)
    def _():
        out_rows[:, :D] = acc[...].astype(BF)
        out_rows[:, D:] = dot_columns(dots[...])
        place_rows(order, out_rows, grad_all, sems)


def grad_pass(weights, fac, block, dots, order, grad_all):
    rows = dots.shape[0]
    return pl.pallas_call(
        functools.partial(grad_kernel, order),
        grid=(NF,),
        in_specs=[
            pl.BlockSpec((D, FB), lambda f: (0, f)),
            pl.BlockSpec((D, FB), lambda f: (0, f + NF)),
            pl.BlockSpec((rows, FB), lambda f: (block, f)),
            pl.BlockSpec((rows, FB), lambda f: (block, f + NF)),
            pl.BlockSpec((rows, 128), lambda f: (0, 0)),
            ANY,
        ],
        out_specs=ANY,
        out_shape=jax.ShapeDtypeStruct(grad_all.shape, BF),
        scratch_shapes=[
            pltpu.VMEM((rows, D), F32),
            pltpu.VMEM((rows, D + EXTRA), BF),
            pltpu.SemaphoreType.DMA((rows // CAP,)),
        ],
        input_output_aliases={5: 0},
        cost_estimate=cost(4 * rows * D * F, D * 2 * F * 2),
        compiler_params=params(20),
    )(weights, weights, fac, fac, dots, grad_all)


def parts_kernel(counts, *refs):
    n = len(counts)
    fac = refs[n][...]
    adds, outs = refs[n + 1 : n + 1 + sum(counts)], refs[-n:]
    for i, count in enumerate(counts):
        total = lax.dot_general(refs[i][...], fac, TN, preferred_element_type=F32)
        for ref in adds[:count]:
            total += ref[...].astype(F32)
        adds = adds[count:]
        outs[i][...] = total.astype(outs[i].dtype)


def parts(xs, fac, plan, dtype, adds=None, into=None, weight=1):
    n, steps = len(plan), len(plan[0])
    adds = adds or [()] * n

    def pick(values):
        def at(f):
            index = values[-1]
            for i in range(steps - 2, -1, -1):
                index = jnp.where(f == i, values[i], index)
            return 0, index

        return at

    def side(first):
        return pl.BlockSpec((256, F), lambda f: (0, f + first))

    flat = [add for some in adds for add in some]
    held = [] if into is None or into is True else [into]
    group, total = (0, steps) if into is None else (plan[0][0][1], 3)
    return pl.pallas_call(
        functools.partial(parts_kernel, [len(some) for some in adds]),
        grid=(steps,),
        in_specs=[pl.BlockSpec((ROWS, 256), pick([b for b, _ in column])) for column in plan]
        + [pl.BlockSpec((ROWS, F), pick([g for _, g in plan[0]]))]
        + [side(first) for _, first in flat]
        + [ANY] * len(held),
        out_specs=[side(group)] * n,
        out_shape=[jax.ShapeDtypeStruct((256, F * total), dtype)] * n,
        input_output_aliases={n + 1 + len(flat): 0} if held else {},
        cost_estimate=cost(weight * 2 * n * ROWS * 256 * steps * F, 2 * ROWS * steps * F),
        compiler_params=params(16),
    )(*([xs] * n), fac, *[value for value, _ in flat], *held)


def weight_grads_of(xs, fac, finish):
    far = parts(xs, fac, [[(4, 0)], [(5, 0)]], BF)
    far_r, far_l, xs, fac = together((*far, xs, fac))
    far_r, far_l = x_shift(far_r, 1), x_shift(far_l, -1)
    near = parts(
        xs,
        fac,
        [
            [(4, 1), (12, 2), (3, 0), (3, 1), (11, 2)],
            [(5, 1), (13, 2), (6, 0), (6, 1), (14, 2)],
        ],
        BF,
    )
    *near, fac = together((*near, fac))
    near_r, near_l = together((x_shift(near[0], 1), x_shift(near[1], -1)))
    far_r, far_l, free = together((far_r, far_l, fac))
    rows = finish(free)
    last = parts(xs, fac, [[(2, 0)], [(7, 0)]], BF, [[(far_r, 0)], [(far_l, 0)]], None, 100000)
    lasts = [together((x_shift(last[0], 1), x_shift(last[1], -1)))]
    for group, block in ((1, 0), (2, 8)):
        last = parts(
            xs,
            fac,
            [[(2 + block, group)], [(7 + block, group)]],
            BF,
            [[(near_r, group - 1)], [(near_l, group - 1)]],
        )
        lasts.append(together((x_shift(last[0], 1), x_shift(last[1], -1))))
    result = True
    for group, block in ((0, 0), (1, 0), (2, 8)):
        last_r, last_l = lasts[group]
        beside = 2 + group
        (over,) = parts(
            xs, fac, [[(1 + block, group)]], BF, [[(near_r, beside), (last_l, 0)]]
        )
        swapped = y_swap(over)
        adds = [[(near_l, beside), (last_r, 0), (swapped, 0)]]
        (result,) = parts(xs, fac, [[(block, group)]], F32, adds, result)
    return result, rows


def home_kernel(routes, probs, back, grads_out, probs_out):
    lane = lax.broadcasted_iota(I32, (T, ROWS), 1)
    expert = (lane // CAP).astype(F32)
    place = (lane % CAP).astype(F32)
    r = columns(routes[...])
    one, two = slots(r[:, 0:1], r[:, 1:2], expert, place)
    both = (one + two).astype(BF)
    grads_out[...] = jnp.dot(both, back[:, :D], preferred_element_type=F32).astype(BF)
    first = jnp.dot(one.astype(BF), back[:, D:], preferred_element_type=F32)
    second = jnp.dot(two.astype(BF), back[:, D:], preferred_element_type=F32)
    sums = [jnp.sum(first.T, axis=0, keepdims=True), jnp.sum(second.T, axis=0, keepdims=True)]
    probs_out[...] = jnp.concatenate(sums, axis=0) / probs[...].astype(F32)


def home_sums(routes, probs, back):
    return pl.pallas_call(
        home_kernel,
        out_shape=[jax.ShapeDtypeStruct((T, D), BF), jax.ShapeDtypeStruct((2, T), F32)],
        cost_estimate=cost(2 * ROWS * T * D, 2 * ROWS * D),
        compiler_params=params(16),
    )(routes.T, probs.T, back)


def shards(tokens, routes, gate_probs, cotangent, expert_weights):
    weights = expert_weights[0]

    home = pack(tokens, cotangent, routes, gate_probs)
    ahead, behind = [home], [home]
    for _ in range(2):
        ahead.append(z_shift(ahead[-1], 1))
        behind.append(z_shift(behind[-1], -1))

    def exchange(messages):
        return [messages[0]] + [plane_swap(messages[j], j) for j in range(1, NQ)]

    def order(ds):
        return [(d, j) for j in range(NQ) for d in ds]

    every = tuple(range(NQ))
    sel_a = select([(i, 0, every, i * CAP) for i in range(3)], [home, ahead[1], behind[1]])
    got_a = exchange(sel_a)
    halfway = [(0, 2, (0, 1), 2 * CAP), (1, -2, (2, 3), 2 * CAP)]
    pair = [(i, 0, every, i * CAP) for i in range(2)]
    got_b = exchange(select(pair + halfway, [ahead[2], behind[2]]))
    two_l, got_a = together((behind[2], got_a))
    three_r, three_l = z_shift(ahead[2], 1), z_shift(two_l, -1)
    held = expert_pass(weights, got_a, [3 * CAP] * NQ, order((0, -1, 1)), 0, (), True)
    three_r, three_l, held, got_b = together((three_r, three_l, held, got_b))
    got_c = exchange(select(pair, [three_r, three_l]))
    across = [piece[2 * CAP :] for piece in got_b]
    four_r = z_shift(jnp.concatenate(across[:2], axis=0), 2)
    four_l = z_shift(jnp.concatenate(across[2:], axis=0), -2)
    held = expert_pass(weights, got_b, [2 * CAP] * NQ, order((-2, 2)), 3, held, True)
    last = order((-3, 3)) + order((4,))
    pieces = got_c + [four_r, four_l]
    xs, fac, dots = expert_pass(weights, pieces, [2 * CAP] * 6, last, 1, held[:2], False)
    weight_grads, rows = weight_grads_of(
        xs, fac, lambda f: grad_pass(weights, f, 1, dots, last, held[2])
    )

    back = lax.all_to_all(
        rows.reshape(32, CAP, D + EXTRA), "expert", split_axis=0, concat_axis=0, tiled=True
    ).reshape(ROWS, D + EXTRA)
    token_grads, prob_grads = home_sums(routes, gate_probs, back)
    return token_grads, prob_grads.T, weight_grads[None]


def solution(mesh):
    rows = P(("dp", "expert"), None)
    return jax.shard_map(
        shards,
        mesh=mesh,
        in_specs=(rows, rows, rows, rows, P("expert", None, None)),
        out_specs=(rows, rows, P("expert", "dp", None)),
        check_vma=False,
    )
```

profile of v0, /device:TPU:1, one launch (start us, length us, event | category | flops | bytes accessed | tf_op | source)
XLA Modules:
  0.0 216.5 jit_solution(12845703297674185169)
XLA Ops:
  4.3 6.5 %collective-permute-start.3 = (bf16[128,4224]{1,0:T(8,128)(2,1)S(1)}, bf16[128,4224]{1,0:T(8,128)(2,1)S(1)}, u32[]{:S(2)}, u32[]{:S(2)}) collective-permute-start(bf16[128,4224]{1,0:T(8,128)(2,1)S(1)} %shard_map.76.refs_0_.refs_3_), channel_id=1, source_target_pairs={{0,28},{1,29},{2,30},{3,31},{4,0},{5,1},{6,2},{7,3},{8,4},{9,5},{1... | collective-permute-start | bytes 3244040 | tf_op jit(solution)/shard_map/ppermute | solution.py:31
  10.8 22.5 %collective-permute-done.3.refs_2_.refs_5_ = bf16[128,4224]{1,0:T(8,128)(2,1)S(1)} collective-permute-done((bf16[128,4224]{1,0:T(8,128)(2,1)S(1)}, bf16[128,4224]{1,0:T(8,128)(2,1)S(1)}, u32[]{:S(2)}, u32[]{:S(2)}) %collective-permute-start.3) | collective-permute-done | bytes 1081376 | tf_op jit(solution)/shard_map/ppermute | solution.py:31
  33.3 3.4 %collective-permute-start.4 = (bf16[128,4224]{1,0:T(8,128)(2,1)S(1)}, bf16[128,4224]{1,0:T(8,128)(2,1)S(1)}, u32[]{:S(2)}, u32[]{:S(2)}) collective-permute-start(bf16[128,4224]{1,0:T(8,128)(2,1)S(1)} %collective-permute-done.3.refs_2_.refs_5_), channel_id=1, source_target_pairs={{0,28},{1,29},{2,30},{3,31},{4,0},{5,1},{6,2},{7,3},{8,4},{9,5},{1... | collective-permute-start | bytes 3244040 | tf_op jit(solution)/shard_map/ppermute | solution.py:31
  36.8 2.4 %shard_map.77 = (bf16[48,4096]{1,0:T(8,128)(2,1)S(1)}, bf16[48,4096]{1,0:T(8,128)(2,1)S(1)}, bf16[48,4096]{1,0:T(8,128)(2,1)S(1)}, bf16[48,4096]{1,0:T(8,128)(2,1)S(1)}) custom-call(bf16[128,4224]{1,0:T(8,128)(2,1)S(1)} %shard_map.76.refs_0_.refs_3_, bf16[128,4224]{1,0:T(8,128)(2,1)S(1)} %collective-permute-done.refs_1_.refs_4_, ...), custom_call_target="tpu_custom_call" | custom-call | flops 196608 | bytes 4608 | tf_op jit(solution)/shard_map/pallas_call | solution.py:120
  41.1 2.9 %collective-permute-start.6 = (bf16[48,4096]{1,0:T(8,128)(2,1)S(1)}, bf16[48,4096]{1,0:T(8,128)(2,1)S(1)}, u32[]{:S(2)}, u32[]{:S(2)}) collective-permute-start(bf16[48,4096]{1,0:T(8,128)(2,1)S(1)} %get-tuple-element.70), channel_id=1, source_target_pairs={{0,2},{1,3},{2,0},{3,1},{4,6},{5,7},{6,4},{7,5},{8,10},{9,11},{10,... | collective-permute-start | bytes 1179656 | tf_op jit(solution)/shard_map/ppermute | solution.py:35
  44.3 8.9 %collective-permute-done.6.refs_2_ = bf16[48,4096]{1,0:T(8,128)(2,1)S(1)} collective-permute-done((bf16[48,4096]{1,0:T(8,128)(2,1)S(1)}, bf16[48,4096]{1,0:T(8,128)(2,1)S(1)}, u32[]{:S(2)}, u32[]{:S(2)}) %collective-permute-start.6) | collective-permute-done | bytes 393248 | tf_op jit(solution)/shard_map/ppermute | solution.py:35
  53.3 8.6 %collective-permute-done.7.refs_3_ = bf16[48,4096]{1,0:T(8,128)(2,1)S(1)} collective-permute-done((bf16[48,4096]{1,0:T(8,128)(2,1)S(1)}, bf16[48,4096]{1,0:T(8,128)(2,1)S(1)}, u32[]{:S(2)}, u32[]{:S(2)}) %collective-permute-start.7) | collective-permute-done | bytes 393248 | tf_op jit(solution)/shard_map/ppermute | solution.py:35
  61.9 2.9 %collective-permute-start.8 = (bf16[128,4224]{1,0:T(8,128)(2,1)S(1)}, bf16[128,4224]{1,0:T(8,128)(2,1)S(1)}, u32[]{:S(2)}, u32[]{:S(2)}) collective-permute-start(bf16[128,4224]{1,0:T(8,128)(2,1)S(1)} %collective-permute-done.4.refs_1_.refs_3_), channel_id=1, source_target_pairs={{0,28},{1,29},{2,30},{3,31},{4,0},{5,1},{6,2},{7,3},{8,4},{9,5},{1... | collective-permute-start | bytes 3244040 | tf_op jit(solution)/shard_map/ppermute | solution.py:31
  64.8 2.3 %shard_map.79 = (bf16[48,4096]{1,0:T(8,128)(2,1)S(1)}, bf16[48,4096]{1,0:T(8,128)(2,1)S(1)}, bf16[48,4096]{1,0:T(8,128)(2,1)S(1)}, bf16[48,4096]{1,0:T(8,128)(2,1)S(1)}) custom-call(bf16[128,4224]{1,0:T(8,128)(2,1)S(1)} %collective-permute-done.1.refs_0_.refs_2_, bf16[128,4224]{1,0:T(8,128)(2,1)S(1)} %collective-permute-done.4.refs_1_.refs_3_, ...), custom_call_target="tpu_custom_call" | custom-call | flops 131072 | bytes 3072 | tf_op jit(solution)/shard_map/pallas_call | solution.py:120
  67.7 2.9 %collective-permute-start.10 = (bf16[48,4096]{1,0:T(8,128)(2,1)S(1)}, bf16[48,4096]{1,0:T(8,128)(2,1)S(1)}, u32[]{:S(2)}, u32[]{:S(2)}) collective-permute-start(bf16[48,4096]{1,0:T(8,128)(2,1)S(1)} %get-tuple-element.82), channel_id=1, source_target_pairs={{0,2},{1,3},{2,0},{3,1},{4,6},{5,7},{6,4},{7,5},{8,10},{9,11},{10,... | collective-permute-start | bytes 1179656 | tf_op jit(solution)/shard_map/ppermute | solution.py:35
  70.9 8.4 %shard_map.78 = (bf16[512,4096]{1,0:T(8,128)(2,1)S(1)}, bf16[512,2304]{1,0:T(8,128)(2,1)S(1)}, bf16[512,2176]{1,0:T(8,128)(2,1)S(1)}) custom-call(bf16[2048,2304]{1,0:T(8,128)(2,1)S(1)} %bitcast.7, bf16[2048,2304]{1,0:T(8,128)(2,1)S(1)} %bitcast.8, bf16[2048,2304]{1,0:T(8,128)(2,1)S(1)} %bitcast.9, bf16[48,4096]{1,0:T(8,128)(2,1)S(1)} %get-tuple-element.73.refs_0_, ...), custom_call_target="tpu_custom_call" | custom-call | flops 2949120 | bytes 9216 | tf_op jit(solution)/shard_map/pallas_call | solution.py:235
  79.9 8.6 %collective-permute-done.11.refs_3_ = bf16[48,4096]{1,0:T(8,128)(2,1)S(1)} collective-permute-done((bf16[48,4096]{1,0:T(8,128)(2,1)S(1)}, bf16[48,4096]{1,0:T(8,128)(2,1)S(1)}, u32[]{:S(2)}, u32[]{:S(2)}) %collective-permute-start.11) | collective-permute-done | bytes 393248 | tf_op jit(solution)/shard_map/ppermute | solution.py:35
  88.5 2.4 %collective-permute-done.2.refs_0_.refs_2_ = bf16[128,4224]{1,0:T(8,128)(2,1)S(1)} collective-permute-done((bf16[128,4224]{1,0:T(8,128)(2,1)S(1)}, bf16[128,4224]{1,0:T(8,128)(2,1)S(1)}, u32[]{:S(2)}, u32[]{:S(2)}) %collective-permute-start.2) | collective-permute-done | bytes 1081376 | tf_op jit(solution)/shard_map/ppermute | solution.py:31
  91.1 2.4 %collective-permute-start.15 = (bf16[32,4096]{1,0:T(8,128)(2,1)S(1)}, bf16[32,4096]{1,0:T(8,128)(2,1)S(1)}, u32[]{:S(2)}, u32[]{:S(2)}) collective-permute-start(bf16[32,4096]{1,0:T(8,128)(2,1)S(1)} %pad_maximum_fusion), channel_id=1, source_target_pairs={{0,8},{1,9},{2,10},{3,11},{4,12},{5,13},{6,14},{7,15},{8,16},{9,17... | collective-permute-start | bytes 786440 | tf_op jit(solution)/shard_map/ppermute | solution.py:31
  95.5 2.0 collective-permute-start.12
  97.5 2.9 %collective-permute-start.13 = (bf16[32,4096]{1,0:T(8,128)(2,1)S(1)}, bf16[32,4096]{1,0:T(8,128)(2,1)S(1)}, u32[]{:S(2)}, u32[]{:S(2)}) collective-permute-start(bf16[32,4096]{1,0:T(8,128)(2,1)S(1)} %get-tuple-element.88), channel_id=1, source_target_pairs={{0,2},{1,3},{2,0},{3,1},{4,6},{5,7},{6,4},{7,5},{8,10},{9,11},{10,... | collective-permute-start | bytes 786440 | tf_op jit(solution)/shard_map/ppermute | solution.py:35
  100.7 6.6 %shard_map.81 = (bf16[512,4096]{1,0:T(8,128)(2,1)S(1)}, bf16[512,2304]{1,0:T(8,128)(2,1)S(1)}, bf16[512,2176]{1,0:T(8,128)(2,1)S(1)}) custom-call(bf16[2048,2304]{1,0:T(8,128)(2,1)S(1)} %bitcast.10, bf16[2048,2304]{1,0:T(8,128)(2,1)S(1)} %bitcast.11, bf16[2048,2304]{1,0:T(8,128)(2,1)S(1)} %bitcast.12, ...), custom_call_target="tpu_custom_call", output_to_operand_aliasing={{0}: (7, {}), {1}: (8, {}), {2}: (9, {})} | custom-call | flops 1966080 | bytes 9216 | tf_op jit(solution)/shard_map/pallas_call | solution.py:235
  107.4 5.2 %collective-permute-done.14.refs_3_ = bf16[32,4096]{1,0:T(8,128)(2,1)S(1)} collective-permute-done((bf16[32,4096]{1,0:T(8,128)(2,1)S(1)}, bf16[32,4096]{1,0:T(8,128)(2,1)S(1)}, u32[]{:S(2)}, u32[]{:S(2)}) %collective-permute-start.14) | collective-permute-done | bytes 262176 | tf_op jit(solution)/shard_map/ppermute | solution.py:35
  112.6 3.8 %shard_map.82 = (bf16[512,4096]{1,0:T(8,128)(2,1)S(1)}, bf16[512,2304]{1,0:T(8,128)(2,1)S(1)}, f32[192,128]{1,0:T(8,128)S(1)}) custom-call(bf16[2048,2304]{1,0:T(8,128)(2,1)S(1)} %bitcast.13, bf16[2048,2304]{1,0:T(8,128)(2,1)S(1)} %bitcast.14, bf16[2048,2304]{1,0:T(8,128)(2,1)S(1)} %bitcast.15, ...), custom_call_target="tpu_custom_call", output_to_operand_aliasing={{0}: (9, {}), {1}: (10, {})} | custom-call | flops 1769472 | bytes 9216 | tf_op jit(solution)/shard_map/pallas_call | solution.py:235
  119.9 4.6 %shard_map.84 = (bf16[256,3840]{1,0:T(8,128)(2,1)}, bf16[256,3840]{1,0:T(8,128)(2,1)}) custom-call(bf16[512,4096]{1,0:T(8,128)(2,1)S(1)} %get-tuple-element.105.refs_0_.refs_1_, bf16[512,4096]{1,0:T(8,128)(2,1)S(1)} %get-tuple-element.105.refs_0_.refs_1_, bf16[512,2304]{1,0:T(8,128)(2,1)S(1)} %get-tuple-element.110.refs_2_.gate_f.up_f.refs_1_), custom_call_target="tpu_custom_call" | custom-call | flops 1966080 | bytes 3840 | tf_op jit(solution)/shard_map/pallas_call | solution.py:328
  124.4 2.7 %collective-permute-start.20 = (bf16[256,3840]{1,0:T(8,128)(2,1)}, bf16[256,3840]{1,0:T(8,128)(2,1)}, u32[]{:S(2)}, u32[]{:S(2)}) collective-permute-start(bf16[256,3840]{1,0:T(8,128)(2,1)} %get-tuple-element.116), channel_id=1, source_target_pairs={{0,192},{32,224},{64,0},{96,32},{128,64},{160,96},{192,128},{224,1... | collective-permute-start | bytes 5898248 | tf_op jit(solution)/shard_map/ppermute | solution.py:39
  128.9 4.5 %shard_map.85 = bf16[512,2176]{1,0:T(8,128)(2,1)S(1)} custom-call(bf16[2048,2304]{1,0:T(8,128)(2,1)S(1)} %bitcast.16, bf16[2048,2304]{1,0:T(8,128)(2,1)S(1)} %bitcast.17, bf16[512,2304]{1,0:T(8,128)(2,1)S(1)} %get-tuple-element.110.refs_2_.gate_f.up_f.refs_1_, ...), custom_call_target="tpu_custom_call", output_to_operand_aliasing={{}: (5, {})} | custom-call | flops 1179648 | bytes 6144 | tf_op jit(solution)/shard_map/pallas_call | solution.py:273
  134.8 7.6 %all-to-all-start = ((bf16[32,16,2176]{2,1,0:T(8,128)(2,1)}), bf16[32,16,2176]{2,1,0:T(8,128)(2,1)}, u32[]{:S(2)}, u32[]{:S(2)}) async-start(bf16[32,16,2176]{2,1,0:T(8,128)(2,1)} %bitcast.18), calls=%async_computation | async-start | bytes 4456448 | tf_op jit(solution)/shard_map/all_to_all | solution.py:444
  142.4 2.2 %copy-done.2 = bf16[512,4096]{1,0:T(8,128)(2,1)S(1)} copy-done((bf16[512,4096]{1,0:T(8,128)(2,1)S(1)}, bf16[512,4096]{1,0:T(8,128)(2,1)}, u32[]{:S(2)}) %copy-start.2) | copy-done | bytes 4194328
  148.1 23.0 %collective-permute-done.19.refs_3_.refs_2_ = bf16[256,3840]{1,0:T(8,128)(2,1)} collective-permute-done((bf16[256,3840]{1,0:T(8,128)(2,1)}, bf16[256,3840]{1,0:T(8,128)(2,1)}, u32[]{:S(2)}, u32[]{:S(2)}) %collective-permute-start.19) | collective-permute-done | bytes 1966112 | tf_op jit(solution)/shard_map/ppermute | solution.py:39
  183.6 4.4 %collective-permute-done.24.refs_3_ = bf16[256,768]{1,0:T(8,128)(2,1)S(1)} collective-permute-done((bf16[256,768]{1,0:T(8,128)(2,1)S(1)}, bf16[256,768]{1,0:T(8,128)(2,1)S(1)}, u32[]{:S(2)}, u32[]{:S(2)}) %collective-permute-start.24) | collective-permute-done | bytes 393248 | tf_op jit(solution)/shard_map/ppermute | solution.py:39
  190.8 5.5 %collective-permute-done.21.refs_3_ = bf16[256,768]{1,0:T(8,128)(2,1)S(1)} collective-permute-done((bf16[256,768]{1,0:T(8,128)(2,1)S(1)}, bf16[256,768]{1,0:T(8,128)(2,1)S(1)}, u32[]{:S(2)}, u32[]{:S(2)}) %collective-permute-start.21) | collective-permute-done | bytes 393248 | tf_op jit(solution)/shard_map/ppermute | solution.py:39
  199.1 2.4 %shard_map.93.refs_5_ = f32[256,2304]{1,0:T(8,128)} custom-call(bf16[512,4096]{1,0:T(8,128)(2,1)S(1)} %copy-done.2, bf16[512,2304]{1,0:T(8,128)(2,1)S(1)} %get-tuple-element.110.refs_2_.gate_f.up_f.refs_1_, bf16[256,3840]{1,0:T(8,128)(2,1)} %collective-permute-done.20.refs_4_.refs_2_, bf16[256,768]{1,0:T(8,128)(2,1)S(1)} %collective-permute-done.27.refs_3_, ...), custom_call_target="tpu_custom_call" | custom-call | flops 196608 | bytes 768 | tf_op jit(solution)/shard_map/pallas_call | solution.py:328
  202.5 2.4 %shard_map.94.refs_5_ = f32[256,2304]{1,0:T(8,128)} custom-call(bf16[512,4096]{1,0:T(8,128)(2,1)S(1)} %copy-done.2, bf16[512,2304]{1,0:T(8,128)(2,1)S(1)} %get-tuple-element.110.refs_2_.gate_f.up_f.refs_1_, bf16[256,3840]{1,0:T(8,128)(2,1)} %collective-permute-done.20.refs_4_.refs_2_, ...), custom_call_target="tpu_custom_call", output_to_operand_aliasing={{}: (5, {})} | custom-call | flops 196608 | bytes 768 | tf_op jit(solution)/shard_map/pallas_call | solution.py:328
  204.9 6.0 %collective-permute-done.23.refs_4_ = bf16[256,768]{1,0:T(8,128)(2,1)S(1)} collective-permute-done((bf16[256,768]{1,0:T(8,128)(2,1)S(1)}, bf16[256,768]{1,0:T(8,128)(2,1)S(1)}, u32[]{:S(2)}, u32[]{:S(2)}) %collective-permute-start.23) | collective-permute-done | bytes 393248 | tf_op jit(solution)/shard_map/ppermute | solution.py:43
  210.9 2.4 %shard_map.95 = f32[256,2304]{1,0:T(8,128)} custom-call(bf16[512,4096]{1,0:T(8,128)(2,1)S(1)} %copy-done.2, bf16[512,2304]{1,0:T(8,128)(2,1)S(1)} %get-tuple-element.110.refs_2_.gate_f.up_f.refs_1_, bf16[256,3840]{1,0:T(8,128)(2,1)} %collective-permute-done.20.refs_4_.refs_2_, ...), custom_call_target="tpu_custom_call", output_to_operand_aliasing={{}: (5, {})} | custom-call | flops 196608 | bytes 768 | tf_op jit(solution)/shard_map/pallas_call | solution.py:328
  213.3 3.2 %shard_map.86 = (bf16[128,2048]{1,0:T(8,128)(2,1)}, f32[2,128]{1,0:T(2,128)}) custom-call(s32[2,128]{1,0:T(2,128)S(1)} %bitcast.20, bf16[2,128]{1,0:T(2,128)(2,1)S(1)} %bitcast.22, bf16[512,2176]{1,0:T(8,128)(2,1)} %bitcast.4.back), custom_call_target="tpu_custom_call" | custom-call | flops 262144 | bytes 2048 | tf_op jit(solution)/shard_map/pallas_call | solution.py:399
  (76 shorter events, 38.9 us)
Async XLA Ops:
  4.3 29.0 %collective-permute-start.3 = (bf16[128,4224]{1,0:T(8,128)(2,1)S(1)}, bf16[128,4224]{1,0:T(8,128)(2,1)S(1)}, u32[]{:S(2)}, u32[]{:S(2)}) collective-permute-start(bf16[128,4224]{1,0:T(8,128)(2,1)S(1)} %shard_map.76.refs_0_.refs_3_), channel_id=1, source_target_pairs={{0,28},{1,29},{2,30},{3,31},{4,0},{5,1},{6,2},{7,3},{8,4},{9,5},{1... | collective-permute-start | bytes 3244040 | tf_op jit(solution)/shard_map/ppermute | solution.py:31
  10.8 25.9 %collective-permute-start = (bf16[128,4224]{1,0:T(8,128)(2,1)S(1)}, bf16[128,4224]{1,0:T(8,128)(2,1)S(1)}, u32[]{:S(2)}, u32[]{:S(2)}) collective-permute-start(bf16[128,4224]{1,0:T(8,128)(2,1)S(1)} %shard_map.76.refs_0_.refs_3_), channel_id=1, source_target_pairs={{0,4},{1,5},{2,6},{3,7},{4,8},{5,9},{6,10},{7,11},{8,12},{9,13},{1... | collective-permute-start | bytes 3244040 | tf_op jit(solution)/shard_map/ppermute | solution.py:31
  33.3 28.5 %collective-permute-start.4 = (bf16[128,4224]{1,0:T(8,128)(2,1)S(1)}, bf16[128,4224]{1,0:T(8,128)(2,1)S(1)}, u32[]{:S(2)}, u32[]{:S(2)}) collective-permute-start(bf16[128,4224]{1,0:T(8,128)(2,1)S(1)} %collective-permute-done.3.refs_2_.refs_5_), channel_id=1, source_target_pairs={{0,28},{1,29},{2,30},{3,31},{4,0},{5,1},{6,2},{7,3},{8,4},{9,5},{1... | collective-permute-start | bytes 3244040 | tf_op jit(solution)/shard_map/ppermute | solution.py:31
  36.8 28.0 %collective-permute-start.1 = (bf16[128,4224]{1,0:T(8,128)(2,1)S(1)}, bf16[128,4224]{1,0:T(8,128)(2,1)S(1)}, u32[]{:S(2)}, u32[]{:S(2)}) collective-permute-start(bf16[128,4224]{1,0:T(8,128)(2,1)S(1)} %collective-permute-done.refs_1_.refs_4_), channel_id=1, source_target_pairs={{0,4},{1,5},{2,6},{3,7},{4,8},{5,9},{6,10},{7,11},{8,12},{9,13},{1... | collective-permute-start | bytes 3244040 | tf_op jit(solution)/shard_map/ppermute | solution.py:31
  36.8 34.2 %copy-start = (bf16[1,2048,2304]{2,1,0:T(8,128)(2,1)S(1)}, bf16[1,2048,2304]{2,1,0:T(8,128)(2,1)}, u32[]{:S(2)}) copy-start(bf16[1,2048,2304]{2,1,0:T(8,128)(2,1)} %param.9) | copy-start | bytes 28311556
  39.2 5.2 %collective-permute-start.5 = (bf16[48,4096]{1,0:T(8,128)(2,1)S(1)}, bf16[48,4096]{1,0:T(8,128)(2,1)S(1)}, u32[]{:S(2)}, u32[]{:S(2)}) collective-permute-start(bf16[48,4096]{1,0:T(8,128)(2,1)S(1)} %get-tuple-element.69), channel_id=1, source_target_pairs={{0,1},{1,0},{2,3},{3,2},{4,5},{5,4},{6,7},{7,6},{8,9},{9,8},{10,11... | collective-permute-start | bytes 1179656 | tf_op jit(solution)/shard_map/ppermute | solution.py:35
  41.1 12.2 %collective-permute-start.6 = (bf16[48,4096]{1,0:T(8,128)(2,1)S(1)}, bf16[48,4096]{1,0:T(8,128)(2,1)S(1)}, u32[]{:S(2)}, u32[]{:S(2)}) collective-permute-start(bf16[48,4096]{1,0:T(8,128)(2,1)S(1)} %get-tuple-element.70), channel_id=1, source_target_pairs={{0,2},{1,3},{2,0},{3,1},{4,6},{5,7},{6,4},{7,5},{8,10},{9,11},{10,... | collective-permute-start | bytes 1179656 | tf_op jit(solution)/shard_map/ppermute | solution.py:35
  44.0 17.9 %collective-permute-start.7 = (bf16[48,4096]{1,0:T(8,128)(2,1)S(1)}, bf16[48,4096]{1,0:T(8,128)(2,1)S(1)}, u32[]{:S(2)}, u32[]{:S(2)}) collective-permute-start(bf16[48,4096]{1,0:T(8,128)(2,1)S(1)} %get-tuple-element.71), channel_id=1, source_target_pairs={{0,3},{1,2},{2,1},{3,0},{4,7},{5,6},{6,5},{7,4},{8,11},{9,10},{10,... | collective-permute-start | bytes 1179656 | tf_op jit(solution)/shard_map/ppermute | solution.py:35
  61.9 26.6 %collective-permute-start.8 = (bf16[128,4224]{1,0:T(8,128)(2,1)S(1)}, bf16[128,4224]{1,0:T(8,128)(2,1)S(1)}, u32[]{:S(2)}, u32[]{:S(2)}) collective-permute-start(bf16[128,4224]{1,0:T(8,128)(2,1)S(1)} %collective-permute-done.4.refs_1_.refs_3_), channel_id=1, source_target_pairs={{0,28},{1,29},{2,30},{3,31},{4,0},{5,1},{6,2},{7,3},{8,4},{9,5},{1... | collective-permute-start | bytes 3244040 | tf_op jit(solution)/shard_map/ppermute | solution.py:31
  64.8 26.1 %collective-permute-start.2 = (bf16[128,4224]{1,0:T(8,128)(2,1)S(1)}, bf16[128,4224]{1,0:T(8,128)(2,1)S(1)}, u32[]{:S(2)}, u32[]{:S(2)}) collective-permute-start(bf16[128,4224]{1,0:T(8,128)(2,1)S(1)} %collective-permute-done.1.refs_0_.refs_2_), channel_id=1, source_target_pairs={{0,4},{1,5},{2,6},{3,7},{4,8},{5,9},{6,10},{7,11},{8,12},{9,13},{1... | collective-permute-start | bytes 3244040 | tf_op jit(solution)/shard_map/ppermute | solution.py:31
  67.1 12.3 %collective-permute-start.9 = (bf16[48,4096]{1,0:T(8,128)(2,1)S(1)}, bf16[48,4096]{1,0:T(8,128)(2,1)S(1)}, u32[]{:S(2)}, u32[]{:S(2)}) collective-permute-start(bf16[48,4096]{1,0:T(8,128)(2,1)S(1)} %get-tuple-element.81), channel_id=1, source_target_pairs={{0,1},{1,0},{2,3},{3,2},{4,5},{5,4},{6,7},{7,6},{8,9},{9,8},{10,11... | collective-permute-start | bytes 1179656 | tf_op jit(solution)/shard_map/ppermute | solution.py:35
  67.7 12.2 %collective-permute-start.10 = (bf16[48,4096]{1,0:T(8,128)(2,1)S(1)}, bf16[48,4096]{1,0:T(8,128)(2,1)S(1)}, u32[]{:S(2)}, u32[]{:S(2)}) collective-permute-start(bf16[48,4096]{1,0:T(8,128)(2,1)S(1)} %get-tuple-element.82), channel_id=1, source_target_pairs={{0,2},{1,3},{2,0},{3,1},{4,6},{5,7},{6,4},{7,5},{8,10},{9,11},{10,... | collective-permute-start | bytes 1179656 | tf_op jit(solution)/shard_map/ppermute | solution.py:35
  70.6 17.9 %collective-permute-start.11 = (bf16[48,4096]{1,0:T(8,128)(2,1)S(1)}, bf16[48,4096]{1,0:T(8,128)(2,1)S(1)}, u32[]{:S(2)}, u32[]{:S(2)}) collective-permute-start(bf16[48,4096]{1,0:T(8,128)(2,1)S(1)} %get-tuple-element.83), channel_id=1, source_target_pairs={{0,3},{1,2},{2,1},{3,0},{4,7},{5,6},{6,5},{7,4},{8,11},{9,10},{10,... | collective-permute-start | bytes 1179656 | tf_op jit(solution)/shard_map/ppermute | solution.py:35
  91.0 16.3 %collective-permute-start.16 = (bf16[32,4096]{1,0:T(8,128)(2,1)S(1)}, bf16[32,4096]{1,0:T(8,128)(2,1)S(1)}, u32[]{:S(2)}, u32[]{:S(2)}) collective-permute-start(bf16[32,4096]{1,0:T(8,128)(2,1)S(1)} %pad_maximum_fusion.1), channel_id=1, source_target_pairs={{0,24},{1,25},{2,26},{3,27},{4,28},{5,29},{6,30},{7,31},{8,0},{9,1... | collective-permute-start | bytes 786440 | tf_op jit(solution)/shard_map/ppermute | solution.py:31
  91.1 16.2 %collective-permute-start.15 = (bf16[32,4096]{1,0:T(8,128)(2,1)S(1)}, bf16[32,4096]{1,0:T(8,128)(2,1)S(1)}, u32[]{:S(2)}, u32[]{:S(2)}) collective-permute-start(bf16[32,4096]{1,0:T(8,128)(2,1)S(1)} %pad_maximum_fusion), channel_id=1, source_target_pairs={{0,8},{1,9},{2,10},{3,11},{4,12},{5,13},{6,14},{7,15},{8,16},{9,17... | collective-permute-start | bytes 786440 | tf_op jit(solution)/shard_map/ppermute | solution.py:31
  95.5 11.9 %collective-permute-start.12 = (bf16[32,4096]{1,0:T(8,128)(2,1)S(1)}, bf16[32,4096]{1,0:T(8,128)(2,1)S(1)}, u32[]{:S(2)}, u32[]{:S(2)}) collective-permute-start(bf16[32,4096]{1,0:T(8,128)(2,1)S(1)} %get-tuple-element.87), channel_id=1, source_target_pairs={{0,1},{1,0},{2,3},{3,2},{4,5},{5,4},{6,7},{7,6},{8,9},{9,8},{10,11... | collective-permute-start | bytes 786440 | tf_op jit(solution)/shard_map/ppermute | solution.py:35
  97.5 9.9 %collective-permute-start.13 = (bf16[32,4096]{1,0:T(8,128)(2,1)S(1)}, bf16[32,4096]{1,0:T(8,128)(2,1)S(1)}, u32[]{:S(2)}, u32[]{:S(2)}) collective-permute-start(bf16[32,4096]{1,0:T(8,128)(2,1)S(1)} %get-tuple-element.88), channel_id=1, source_target_pairs={{0,2},{1,3},{2,0},{3,1},{4,6},{5,7},{6,4},{7,5},{8,10},{9,11},{10,... | collective-permute-start | bytes 786440 | tf_op jit(solution)/shard_map/ppermute | solution.py:35
  100.4 12.2 %collective-permute-start.14 = (bf16[32,4096]{1,0:T(8,128)(2,1)S(1)}, bf16[32,4096]{1,0:T(8,128)(2,1)S(1)}, u32[]{:S(2)}, u32[]{:S(2)}) collective-permute-start(bf16[32,4096]{1,0:T(8,128)(2,1)S(1)} %get-tuple-element.89), channel_id=1, source_target_pairs={{0,3},{1,2},{2,1},{3,0},{4,7},{5,6},{6,5},{7,4},{8,11},{9,10},{10,... | collective-permute-start | bytes 786440 | tf_op jit(solution)/shard_map/ppermute | solution.py:35
  117.1 11.8 %collective-permute-start.17 = (bf16[256,768]{1,0:T(8,128)(2,1)S(1)}, bf16[256,768]{1,0:T(8,128)(2,1)S(1)}, u32[]{:S(2)}, u32[]{:S(2)}) collective-permute-start(bf16[256,768]{1,0:T(8,128)(2,1)S(1)} %get-tuple-element.103), channel_id=1, source_target_pairs={{0,64},{32,96},{64,128},{96,160},{128,192},{160,224},{192,0},{224,... | collective-permute-start | bytes 1179656 | tf_op jit(solution)/shard_map/ppermute | solution.py:39
  118.3 10.6 %collective-permute-start.18 = (bf16[256,768]{1,0:T(8,128)(2,1)S(1)}, bf16[256,768]{1,0:T(8,128)(2,1)S(1)}, u32[]{:S(2)}, u32[]{:S(2)}) collective-permute-start(bf16[256,768]{1,0:T(8,128)(2,1)S(1)} %get-tuple-element.104), channel_id=1, source_target_pairs={{0,192},{32,224},{64,0},{96,32},{128,64},{160,96},{192,128},{224,1... | collective-permute-start | bytes 1179656 | tf_op jit(solution)/shard_map/ppermute | solution.py:39
  124.4 46.7 %collective-permute-start.19 = (bf16[256,3840]{1,0:T(8,128)(2,1)}, bf16[256,3840]{1,0:T(8,128)(2,1)}, u32[]{:S(2)}, u32[]{:S(2)}) collective-permute-start(bf16[256,3840]{1,0:T(8,128)(2,1)} %get-tuple-element.115), channel_id=1, source_target_pairs={{0,64},{32,96},{64,128},{96,160},{128,192},{160,224},{192,0},{224,... | collective-permute-start | bytes 5898248 | tf_op jit(solution)/shard_map/ppermute | solution.py:39
  124.4 46.7 %collective-permute-start.20 = (bf16[256,3840]{1,0:T(8,128)(2,1)}, bf16[256,3840]{1,0:T(8,128)(2,1)}, u32[]{:S(2)}, u32[]{:S(2)}) collective-permute-start(bf16[256,3840]{1,0:T(8,128)(2,1)} %get-tuple-element.116), channel_id=1, source_target_pairs={{0,192},{32,224},{64,0},{96,32},{128,64},{160,96},{192,128},{224,1... | collective-permute-start | bytes 5898248 | tf_op jit(solution)/shard_map/ppermute | solution.py:39
  134.8 78.5 %all-to-all-start = ((bf16[32,16,2176]{2,1,0:T(8,128)(2,1)}), bf16[32,16,2176]{2,1,0:T(8,128)(2,1)}, u32[]{:S(2)}, u32[]{:S(2)}) async-start(bf16[32,16,2176]{2,1,0:T(8,128)(2,1)} %bitcast.18), calls=%async_computation | async-start | bytes 4456448 | tf_op jit(solution)/shard_map/all_to_all | solution.py:444
  145.2 34.4 %collective-permute-start.27 = (bf16[256,768]{1,0:T(8,128)(2,1)S(1)}, bf16[256,768]{1,0:T(8,128)(2,1)S(1)}, u32[]{:S(2)}, u32[]{:S(2)}) collective-permute-start(bf16[256,768]{1,0:T(8,128)(2,1)S(1)} %get-tuple-element.129), channel_id=1, source_target_pairs={{0,64},{32,96},{64,128},{96,160},{128,192},{160,224},{192,0},{224,... | collective-permute-start | bytes 1179656 | tf_op jit(solution)/shard_map/ppermute | solution.py:39
  146.5 34.3 %collective-permute-start.28 = (bf16[256,768]{1,0:T(8,128)(2,1)S(1)}, bf16[256,768]{1,0:T(8,128)(2,1)S(1)}, u32[]{:S(2)}, u32[]{:S(2)}) collective-permute-start(bf16[256,768]{1,0:T(8,128)(2,1)S(1)} %get-tuple-element.130), channel_id=1, source_target_pairs={{0,192},{32,224},{64,0},{96,32},{128,64},{160,96},{192,128},{224,1... | collective-permute-start | bytes 1179656 | tf_op jit(solution)/shard_map/ppermute | solution.py:39
  173.0 15.0 %collective-permute-start.24 = (bf16[256,768]{1,0:T(8,128)(2,1)S(1)}, bf16[256,768]{1,0:T(8,128)(2,1)S(1)}, u32[]{:S(2)}, u32[]{:S(2)}) collective-permute-start(bf16[256,768]{1,0:T(8,128)(2,1)S(1)} %get-tuple-element.123), channel_id=1, source_target_pairs={{0,64},{32,96},{64,128},{96,160},{128,192},{160,224},{192,0},{224,... | collective-permute-start | bytes 1179656 | tf_op jit(solution)/shard_map/ppermute | solution.py:39
  173.8 14.2 %collective-permute-start.25 = (bf16[256,768]{1,0:T(8,128)(2,1)S(1)}, bf16[256,768]{1,0:T(8,128)(2,1)S(1)}, u32[]{:S(2)}, u32[]{:S(2)}) collective-permute-start(bf16[256,768]{1,0:T(8,128)(2,1)S(1)} %get-tuple-element.124), channel_id=1, source_target_pairs={{0,192},{32,224},{64,0},{96,32},{128,64},{160,96},{192,128},{224,1... | collective-permute-start | bytes 1179656 | tf_op jit(solution)/shard_map/ppermute | solution.py:39
  177.5 18.8 %collective-permute-start.21 = (bf16[256,768]{1,0:T(8,128)(2,1)S(1)}, bf16[256,768]{1,0:T(8,128)(2,1)S(1)}, u32[]{:S(2)}, u32[]{:S(2)}) collective-permute-start(bf16[256,768]{1,0:T(8,128)(2,1)S(1)} %get-tuple-element.119), channel_id=1, source_target_pairs={{0,64},{32,96},{64,128},{96,160},{128,192},{160,224},{192,0},{224,... | collective-permute-start | bytes 1179656 | tf_op jit(solution)/shard_map/ppermute | solution.py:39
  179.5 16.8 %collective-permute-start.22 = (bf16[256,768]{1,0:T(8,128)(2,1)S(1)}, bf16[256,768]{1,0:T(8,128)(2,1)S(1)}, u32[]{:S(2)}, u32[]{:S(2)}) collective-permute-start(bf16[256,768]{1,0:T(8,128)(2,1)S(1)} %get-tuple-element.120), channel_id=1, source_target_pairs={{0,192},{32,224},{64,0},{96,32},{128,64},{160,96},{192,128},{224,1... | collective-permute-start | bytes 1179656 | tf_op jit(solution)/shard_map/ppermute | solution.py:39
  182.2 16.9 %collective-permute-start.29 = (bf16[256,768]{1,0:T(8,128)(2,1)S(1)}, bf16[256,768]{1,0:T(8,128)(2,1)S(1)}, u32[]{:S(2)}, u32[]{:S(2)}) collective-permute-start(bf16[256,768]{1,0:T(8,128)(2,1)S(1)} %shard_map.92), channel_id=1, source_target_pairs={{0,32},{32,0},{64,96},{96,64},{128,160},{160,128},{192,224},{224,1... | collective-permute-start | bytes 1179656 | tf_op jit(solution)/shard_map/ppermute | solution.py:43
  189.5 13.0 %collective-permute-start.26 = (bf16[256,768]{1,0:T(8,128)(2,1)S(1)}, bf16[256,768]{1,0:T(8,128)(2,1)S(1)}, u32[]{:S(2)}, u32[]{:S(2)}) collective-permute-start(bf16[256,768]{1,0:T(8,128)(2,1)S(1)} %shard_map.90), channel_id=1, source_target_pairs={{0,32},{32,0},{64,96},{96,64},{128,160},{160,128},{192,224},{224,1... | collective-permute-start | bytes 1179656 | tf_op jit(solution)/shard_map/ppermute | solution.py:43
  197.8 13.1 %collective-permute-start.23 = (bf16[256,768]{1,0:T(8,128)(2,1)S(1)}, bf16[256,768]{1,0:T(8,128)(2,1)S(1)}, u32[]{:S(2)}, u32[]{:S(2)}) collective-permute-start(bf16[256,768]{1,0:T(8,128)(2,1)S(1)} %shard_map.88), channel_id=1, source_target_pairs={{0,32},{32,0},{64,96},{96,64},{128,160},{160,128},{192,224},{224,1... | collective-permute-start | bytes 1179656 | tf_op jit(solution)/shard_map/ppermute | solution.py:43
  (9 other events, 27.3 us)
where the time goes:
time: 219 us; the launch traced here: 217 us
  waiting for transfers between devices  101 us (46%)
  Pallas kernels  54.5 us (25%)
  starting transfers between devices  53.5 us (24%)
  local copies, waits for them, and re-layouts  7.05 us (3%)
    ppermute x10, waiting for transfers between devices, x_shift(): lax.ppermute(value, 'dp', [(i, (i + 2 * step) % 8) for i in range(8)])  36.6 us
    ppermute x9, waiting for transfers between devices, plane_swap(): return lax.ppermute(value, 'expert', [(i, i ^ mask) for i in range(32)])  31.9 us
    ppermute x8, waiting for transfers between devices, z_shift(): lax.ppermute(value, 'expert', [(i, (i + NQ * step) % 32) for i in range(3...  25 us
    pallas_call x11, Pallas kernels, parts(): pl.pallas_call(functools.partial(parts_kernel, [len(some) for some in add...  21.1 us
    pallas_call x3, Pallas kernels, expert_pass(): pl.pallas_call(functools.partial(expert_kernel, sizes, order, grads, len(...  18.9 us
    ppermute x8, starting transfers between devices, z_shift(): lax.ppermute(value, 'expert', [(i, (i + NQ * step) % 32) for i in range(3...  15.3 us
    ppermute x9, starting transfers between devices, plane_swap(): return lax.ppermute(value, 'expert', [(i, i ^ mask) for i in range(32)])  14.2 us
    ppermute x10, starting transfers between devices, x_shift(): lax.ppermute(value, 'dp', [(i, (i + 2 * step) % 8) for i in range(8)])  12.4 us
  transfers between devices with their start and end apart: 31, of which 14 were waited for; matrix products, arithmetic and copies ran while one was open for 0% of the time, Pallas kernels for 22%

commit v1 on v0

--- a/solution.py
+++ b/solution.py
@@ -27,8 +27,8 @@
 together = lax.optimization_barrier
 
 
-def z_shift(value, step):
-    return lax.ppermute(value, "expert", [(i, (i + NQ * step) % 32) for i in range(32)])
+def z_shift(value, step, mask=0):
+    return lax.ppermute(value, "expert", [(i, ((i ^ mask) + NQ * step) % 32) for i in range(32)])
 
 
 def plane_swap(value, mask):
@@ -57,21 +57,44 @@
     return lax.dot_general(eye, pairs.astype(F32).astype(BF), NT, preferred_element_type=F32)
 
 
-def pack_kernel(tokens, cotangent, routes, probs, out):
-    out[:, :D] = tokens[...]
-    out[:, D : 2 * D] = cotangent[...]
+def pack_kernel(tokens, cotangent, routes, probs, out, pairs, weights, meta, sems):
+    loads = [
+        pltpu.make_async_copy(routes, pairs, sems.at[0]),
+        pltpu.make_async_copy(probs, weights, sems.at[1]),
+    ]
+    rows = [
+        pltpu.make_async_copy(tokens, out.at[:, pl.ds(0, D)], sems.at[2]),
+        pltpu.make_async_copy(cotangent, out.at[:, pl.ds(D, D)], sems.at[3]),
+    ]
+    for copy in loads + rows:
+        copy.start()
+    for copy in loads:
+        copy.wait()
     lane = lax.broadcasted_iota(I32, (T, EXTRA), 1)
-    r, p = columns(routes[...]), columns(probs[...])
-    meta = jnp.where(lane == 0, r[:, 0:1], jnp.where(lane == 1, r[:, 1:2], 0.0))
-    meta += jnp.where(lane == 2, p[:, 0:1], jnp.where(lane == 3, p[:, 1:2], 0.0))
-    out[:, 2 * D :] = meta.astype(BF)
+    r, p = columns(pairs[...]), columns(weights[...])
+    value = jnp.where(lane == 0, r[:, 0:1], jnp.where(lane == 1, r[:, 1:2], 0.0))
+    value += jnp.where(lane == 2, p[:, 0:1], jnp.where(lane == 3, p[:, 1:2], 0.0))
+    meta[...] = value.astype(BF)
+    last = pltpu.make_async_copy(meta, out.at[:, pl.ds(2 * D, EXTRA)], sems.at[4])
+    last.start()
+    last.wait()
+    for copy in rows:
+        copy.wait()
 
 
 def pack(tokens, cotangent, routes, probs):
     return pl.pallas_call(
         pack_kernel,
+        in_specs=[ANY] * 4,
+        out_specs=ANY,
         out_shape=jax.ShapeDtypeStruct((T, 2 * D + EXTRA), BF),
-        cost_estimate=cost(0, 4 * T * D * 2),
+        scratch_shapes=[
+            pltpu.VMEM((2, T), I32),
+            pltpu.VMEM((2, T), BF),
+            pltpu.VMEM((T, EXTRA), BF),
+            pltpu.SemaphoreType.DMA((5,)),
+        ],
+        cost_estimate=cost(0, 8 * T * D),
         compiler_params=params(8),
     )(tokens, cotangent, routes.T, probs.T)
 
@@ -89,14 +112,15 @@
 
 
 def select_kernel(plan, n, *refs):
-    metas, ins, outs, hot = refs[:n], refs[n : 2 * n], refs[2 * n : -1], refs[-1]
+    metas, ins = refs[:n], refs[n : 2 * n]
+    outs, hot = refs[2 * n : -1], refs[-1]
     c = pl.program_id(0)
 
     @pl.when(c == 0)
     def _():
         me = lax.axis_index("expert")
         z, q = me // NQ, me % NQ
-        for i, (block, step, _, _) in enumerate(plan):
+        for i, (block, step, _) in enumerate(plan):
             lane = lax.broadcasted_iota(I32, (T, NQ * CAP), 1)
             plane = (z + step + NZ) % NZ
             expert = (plane * NQ + jnp.bitwise_xor(q, lane // CAP)).astype(F32)
@@ -106,27 +130,26 @@
             hot[0, i] = (one + two).astype(BF)
             hot[1, i] = (one * meta[:, 2:3] + two * meta[:, 3:4]).astype(BF)
 
-    for i, (block, _, experts, at) in enumerate(plan):
+    for i, (block, _, targets) in enumerate(plan):
         rows = lax.dot_general(hot[c // 2, i], ins[block][...], TN, preferred_element_type=F32)
         rows = rows.astype(BF)
-        for j in experts:
-            outs[j][at : at + CAP, :] = rows[j * CAP : (j + 1) * CAP, :]
-
-
-def select(plan, ins):
+        for j, out, at in targets:
+            outs[out][at : at + CAP, :] = rows[j * CAP : (j + 1) * CAP, :]
+
+
+def select(plan, ins, heights):
     n = len(ins)
     width = 1024
-    height = max(at for _, _, _, at in plan) + CAP
     return pl.pallas_call(
         functools.partial(select_kernel, plan, n),
         grid=(2 * D // width,),
         in_specs=[pl.BlockSpec((T, EXTRA), lambda c: (0, 2 * D // EXTRA))] * n
         + [pl.BlockSpec((T, width), lambda c: (0, c))] * n,
-        out_specs=[pl.BlockSpec((height, width), lambda c: (0, c))] * NQ,
-        out_shape=[jax.ShapeDtypeStruct((height, 2 * D), BF)] * NQ,
+        out_specs=[pl.BlockSpec((height, width), lambda c: (0, c)) for height in heights],
+        out_shape=[jax.ShapeDtypeStruct((height, 2 * D), BF) for height in heights],
         scratch_shapes=[pltpu.VMEM((2, len(plan), T, NQ * CAP), BF)],
         cost_estimate=cost(2 * n * 64 * T * 2 * D, n * 3 * T * D * 2),
-        compiler_params=params(10),
+        compiler_params=params(12),
     )(*ins, *ins)
 
 
@@ -214,7 +237,8 @@
             dots[...] = total
 
 
-def expert_pass(weights, pieces, sizes, order, block, held, grads):
+def expert_pass(weights, pieces, order, block, held, grads):
+    sizes = [size for _, size, _ in pieces]
     rows = sum(sizes)
     whole = lambda f: (0, 0)
     mine = lambda f: (block, 0)
@@ -240,7 +264,7 @@
             pl.BlockSpec((D, FB), lambda f: (0, f + NF)),
             pl.BlockSpec((D, FB), lambda f: (0, f + 2 * NF)),
         ]
-        + [pl.BlockSpec((size, 2 * D), whole) for size in sizes]
+        + [pl.BlockSpec((size, 2 * D), (lambda f, at=at: (at, 0))) for _, size, at in pieces]
         + [ANY] * len(held),
         out_specs=outs,
         out_shape=shapes,
@@ -248,7 +272,7 @@
         input_output_aliases={3 + len(pieces) + i: i for i in range(len(held))},
         cost_estimate=cost(2 * rows * D * (5 if grads else 3) * F, D * 3 * F * 2),
         compiler_params=params(24),
-    )(weights, weights, weights, *pieces, *held)
+    )(weights, weights, weights, *[piece for piece, _, _ in pieces], *held)
 
 
 def grad_kernel(order, gate_w, up_w, gate_f, up_f, dots, held, grad_all, acc, out_rows, sems):
@@ -340,6 +364,31 @@
     )(*([xs] * n), fac, *[value for value, _ in flat], *held)
 
 
+def total_kernel(n, *refs):
+    value = refs[0][...].astype(F32)
+    for ref in refs[1:n]:
+        value += ref[...].astype(F32)
+    refs[-1][...] = value.astype(refs[-1].dtype)
+
+
+def total(adds, dtype, group=0, into=None):
+    n = len(adds)
+    held = [] if into is None or into is True else [into]
+    return pl.pallas_call(
+        functools.partial(total_kernel, n),
+        grid=(2,),
+        in_specs=[
+            pl.BlockSpec((256, F // 2), lambda f, at=at: (0, 2 * at + f)) for _, at in adds
+        ]
+        + [ANY] * len(held),
+        out_specs=pl.BlockSpec((256, F // 2), lambda f: (0, 2 * group + f)),
+        out_shape=jax.ShapeDtypeStruct((256, F if into is None else 3 * F), dtype),
+        input_output_aliases={n: 0} if held else {},
+        cost_estimate=cost(n * 256 * F, n * 512 * F),
+        compiler_params=params(8),
+    )(*[value for value, _ in adds], *held)
+
+
 def weight_grads_of(xs, fac, finish):
     far = parts(xs, fac, [[(4, 0)], [(5, 0)]], BF)
     far_r, far_l, xs, fac = together((*far, xs, fac))
@@ -356,7 +405,7 @@
     *near, fac = together((*near, fac))
     near_r, near_l = together((x_shift(near[0], 1), x_shift(near[1], -1)))
     far_r, far_l, free = together((far_r, far_l, fac))
-    rows = finish(free)
+    homes = finish(free)
     last = parts(xs, fac, [[(2, 0)], [(7, 0)]], BF, [[(far_r, 0)], [(far_l, 0)]], None, 100000)
     lasts = [together((x_shift(last[0], 1), x_shift(last[1], -1)))]
     for group, block in ((1, 0), (2, 8)):
@@ -368,17 +417,17 @@
             [[(near_r, group - 1)], [(near_l, group - 1)]],
         )
         lasts.append(together((x_shift(last[0], 1), x_shift(last[1], -1))))
+    mine, away = parts(xs, fac, [[(0, 0), (0, 1), (8, 2)], [(1, 0), (1, 1), (9, 2)]], BF)
     result = True
-    for group, block in ((0, 0), (1, 0), (2, 8)):
+    for group in range(3):
         last_r, last_l = lasts[group]
-        beside = 2 + group
-        (over,) = parts(
-            xs, fac, [[(1 + block, group)]], BF, [[(near_r, beside), (last_l, 0)]]
-        )
+        over = total([(away, group), (near_r, 2 + group), (last_l, 0)], BF)
         swapped = y_swap(over)
-        adds = [[(near_l, beside), (last_r, 0), (swapped, 0)]]
-        (result,) = parts(xs, fac, [[(block, group)]], F32, adds, result)
-    return result, rows
+        if group == 2:
+            swapped, homes = together((swapped, homes))
+        adds = [(mine, group), (near_l, 2 + group), (last_r, 0), (swapped, 0)]
+        result = total(adds, F32, group, result)
+    return result, homes
 
 
 def home_kernel(routes, probs, back, grads_out, probs_out):
@@ -419,32 +468,52 @@
     def order(ds):
         return [(d, j) for j in range(NQ) for d in ds]
 
-    every = tuple(range(NQ))
-    sel_a = select([(i, 0, every, i * CAP) for i in range(3)], [home, ahead[1], behind[1]])
+    def each(at):
+        return [(j, j, at) for j in range(NQ)]
+
+    def whole_of(pieces, rows):
+        return [(piece, rows, 0) for piece in pieces]
+
+    sel_a = select(
+        [(i, 0, each(i * CAP)) for i in range(3)], [home, ahead[1], behind[1]], [48] * NQ
+    )
     got_a = exchange(sel_a)
-    halfway = [(0, 2, (0, 1), 2 * CAP), (1, -2, (2, 3), 2 * CAP)]
-    pair = [(i, 0, every, i * CAP) for i in range(2)]
-    got_b = exchange(select(pair + halfway, [ahead[2], behind[2]]))
     two_l, got_a = together((behind[2], got_a))
-    three_r, three_l = z_shift(ahead[2], 1), z_shift(two_l, -1)
-    held = expert_pass(weights, got_a, [3 * CAP] * NQ, order((0, -1, 1)), 0, (), True)
-    three_r, three_l, held, got_b = together((three_r, three_l, held, got_b))
-    got_c = exchange(select(pair, [three_r, three_l]))
+    plan = [
+        (0, 0, each(0)),
+        (1, 0, each(CAP)),
+        (0, 2, [(0, 0, 32), (1, 1, 32)]),
+        (1, -2, [(2, 2, 32), (3, 3, 32)]),
+        (0, 1, [(j, 4, j * CAP) for j in range(NQ)]),
+        (1, -1, [(j, 5, j * CAP) for j in range(NQ)]),
+    ]
+    *sel_b, on_r, on_l = select(plan, [ahead[2], two_l], [48] * NQ + [64] * 2)
+    three_r, three_l = z_shift(on_r, 1), z_shift(on_l, -1)
+    got_b = exchange(sel_b)
+    held = expert_pass(weights, whole_of(got_a, 48), order((0, -1, 1)), 0, (), True)
+    three_r, three_l, held = together((three_r, three_l, held))
+    got_c = exchange(
+        [
+            jnp.concatenate([v[j * CAP : (j + 1) * CAP] for v in (three_r, three_l)], axis=0)
+            for j in range(NQ)
+        ]
+    )
     across = [piece[2 * CAP :] for piece in got_b]
     four_r = z_shift(jnp.concatenate(across[:2], axis=0), 2)
     four_l = z_shift(jnp.concatenate(across[2:], axis=0), -2)
-    held = expert_pass(weights, got_b, [2 * CAP] * NQ, order((-2, 2)), 3, held, True)
+    held = expert_pass(weights, whole_of(got_b, 32), order((-2, 2)), 3, held, True)
     last = order((-3, 3)) + order((4,))
-    pieces = got_c + [four_r, four_l]
-    xs, fac, dots = expert_pass(weights, pieces, [2 * CAP] * 6, last, 1, held[:2], False)
-    weight_grads, rows = weight_grads_of(
-        xs, fac, lambda f: grad_pass(weights, f, 1, dots, last, held[2])
-    )
-
-    back = lax.all_to_all(
-        rows.reshape(32, CAP, D + EXTRA), "expert", split_axis=0, concat_axis=0, tiled=True
-    ).reshape(ROWS, D + EXTRA)
-    token_grads, prob_grads = home_sums(routes, gate_probs, back)
+    pieces = whole_of(got_c + [four_r, four_l], 32)
+    xs, fac, dots = expert_pass(weights, pieces, last, 1, held[:2], False)
+    def finish(factors):
+        rows = grad_pass(weights, factors, 1, dots, last, held[2])
+        back = lax.all_to_all(
+            rows.reshape(32, CAP, D + EXTRA), "expert", split_axis=0, concat_axis=0, tiled=True
+        ).reshape(ROWS, D + EXTRA)
+        return home_sums(routes, gate_probs, back)
+
+    weight_grads, homes = weight_grads_of(xs, fac, finish)
+    token_grads, prob_grads = homes
     return token_grads, prob_grads.T, weight_grads[None]
 
 

time: 219 us -> 209 us (0.954)
  waiting for transfers between devices: 101 us -> 90.7 us
    pallas_call x1 -> x7, Pallas kernels: 0.27 us -> 9.85 us  [the longest x6 9.45 us: total(): pl.pallas_call(functools.partial(total_kernel, n), grid=(2,), in_specs=[p...]
    pallas_call x11 -> x6, Pallas kernels: 21.1 us -> 11.8 us  [parts(): pl.pallas_call(functools.partial(parts_kernel, [len(some) for some in add...]
    ppermute x9, waiting for transfers between devices: 31.9 us -> 26.3 us  [plane_swap(): return lax.ppermute(value, 'expert', [(i, i ^ mask) for i in range(32)])]
    ppermute x3, starting transfers between devices: 3.95 us -> 0.28 us  [y_swap(): return lax.ppermute(value, 'dp', [(i, i ^ 1) for i in range(8)])]
    all_to_all x1, starting transfers between devices: 7.58 us -> 11.1 us  [finish(): lax.all_to_all(rows.reshape(32, CAP, D + EXTRA), 'expert', split_axis=0,...]
    ppermute x10, waiting for transfers between devices: 36.6 us -> 33.8 us  [x_shift(): lax.ppermute(value, 'dp', [(i, (i + 2 * step) % 8) for i in range(8)])]
    ppermute x8, waiting for transfers between devices: 25 us -> 22.5 us  [z_shift(): lax.ppermute(value, 'expert', [(i, ((i ^ mask) + NQ * step) % 32) for i i...]
    pallas_call x3 -> x2, Pallas kernels: 6.58 us -> 5.19 us  [select(): pl.pallas_call(functools.partial(select_kernel, plan, n), grid=(2 * D //...]
  transfers between devices with their start and end apart: 31 -> 31, of which waited for: 14 -> 12; matrix products, arithmetic and copies ran while one was open for 0% -> 0% of each run, Pallas kernels for 22% -> 21%
where the time goes in v1:
time: 209 us; the launch traced here: 206 us
  waiting for transfers between devices  90.7 us (43%)
  starting transfers between devices  53.9 us (26%)
  Pallas kernels  53.5 us (26%)
  local copies, waits for them, and re-layouts  7.17 us (3%)
    ppermute x10, waiting for transfers between devices, x_shift(): lax.ppermute(value, 'dp', [(i, (i + 2 * step) % 8) for i in range(8)])  33.8 us
    ppermute x9, waiting for transfers between devices, plane_swap(): return lax.ppermute(value, 'expert', [(i, i ^ mask) for i in range(32)])  26.3 us
    ppermute x8, waiting for transfers between devices, z_shift(): lax.ppermute(value, 'expert', [(i, ((i ^ mask) + NQ * step) % 32) for i i...  22.5 us
    pallas_call x3, Pallas kernels, expert_pass(): pl.pallas_call(functools.partial(expert_kernel, sizes, order, grads, len(...  18.9 us
    ppermute x9, starting transfers between devices, plane_swap(): return lax.ppermute(value, 'expert', [(i, i ^ mask) for i in range(32)])  15.3 us
    ppermute x8, starting transfers between devices, z_shift(): lax.ppermute(value, 'expert', [(i, ((i ^ mask) + NQ * step) % 32) for i i...  15.1 us
    ppermute x10, starting transfers between devices, x_shift(): lax.ppermute(value, 'dp', [(i, (i + 2 * step) % 8) for i in range(8)])  12.2 us
    pallas_call x6, Pallas kernels, parts(): pl.pallas_call(functools.partial(parts_kernel, [len(some) for some in add...  11.8 us
  transfers between devices with their start and end apart: 31, of which 12 were waited for; matrix products, arithmetic and copies ran while one was open for 0% of the time, Pallas kernels for 21%

profile of v1, /device:TPU:1, one launch (start us, length us, event | category | flops | bytes accessed | tf_op | source)
XLA Modules:
  0.0 206.3 jit_solution(2479253493604471488)
XLA Ops:
  4.5 6.5 %collective-permute-start.2 = (bf16[128,4224]{1,0:T(8,128)(2,1)S(1)}, bf16[128,4224]{1,0:T(8,128)(2,1)S(1)}, u32[]{:S(2)}, u32[]{:S(2)}) collective-permute-start(bf16[128,4224]{1,0:T(8,128)(2,1)S(1)} %shard_map.76.refs_0_.refs_3_), channel_id=1, source_target_pairs={{0,28},{1,29},{2,30},{3,31},{4,0},{5,1},{6,2},{7,3},{8,4},{9,5},{1... | collective-permute-start | bytes 3244040 | tf_op jit(solution)/shard_map/ppermute | solution.py:31
  10.9 22.5 %collective-permute-done.2.refs_2_.refs_5_ = bf16[128,4224]{1,0:T(8,128)(2,1)S(1)} collective-permute-done((bf16[128,4224]{1,0:T(8,128)(2,1)S(1)}, bf16[128,4224]{1,0:T(8,128)(2,1)S(1)}, u32[]{:S(2)}, u32[]{:S(2)}) %collective-permute-start.2) | collective-permute-done | bytes 1081376 | tf_op jit(solution)/shard_map/ppermute | solution.py:31
  33.5 3.4 %collective-permute-start.3 = (bf16[128,4224]{1,0:T(8,128)(2,1)S(1)}, bf16[128,4224]{1,0:T(8,128)(2,1)S(1)}, u32[]{:S(2)}, u32[]{:S(2)}) collective-permute-start(bf16[128,4224]{1,0:T(8,128)(2,1)S(1)} %collective-permute-done.2.refs_2_.refs_5_), channel_id=1, source_target_pairs={{0,28},{1,29},{2,30},{3,31},{4,0},{5,1},{6,2},{7,3},{8,4},{9,5},{1... | collective-permute-start | bytes 3244040 | tf_op jit(solution)/shard_map/ppermute | solution.py:31
  36.9 2.4 %shard_map.77 = (bf16[48,4096]{1,0:T(8,128)(2,1)S(1)}, bf16[48,4096]{1,0:T(8,128)(2,1)S(1)}, bf16[48,4096]{1,0:T(8,128)(2,1)S(1)}, bf16[48,4096]{1,0:T(8,128)(2,1)S(1)}) custom-call(bf16[128,4224]{1,0:T(8,128)(2,1)S(1)} %shard_map.76.refs_0_.refs_3_, bf16[128,4224]{1,0:T(8,128)(2,1)S(1)} %collective-permute-done.refs_1_.refs_4_, ...), custom_call_target="tpu_custom_call" | custom-call | flops 196608 | bytes 4608 | tf_op jit(solution)/shard_map/pallas_call | solution.py:143
  41.2 2.9 %collective-permute-start.5 = (bf16[48,4096]{1,0:T(8,128)(2,1)S(1)}, bf16[48,4096]{1,0:T(8,128)(2,1)S(1)}, u32[]{:S(2)}, u32[]{:S(2)}) collective-permute-start(bf16[48,4096]{1,0:T(8,128)(2,1)S(1)} %get-tuple-element.69), channel_id=1, source_target_pairs={{0,2},{1,3},{2,0},{3,1},{4,6},{5,7},{6,4},{7,5},{8,10},{9,11},{10,... | collective-permute-start | bytes 1179656 | tf_op jit(solution)/shard_map/ppermute | solution.py:35
  44.4 8.9 %collective-permute-done.5.refs_2_ = bf16[48,4096]{1,0:T(8,128)(2,1)S(1)} collective-permute-done((bf16[48,4096]{1,0:T(8,128)(2,1)S(1)}, bf16[48,4096]{1,0:T(8,128)(2,1)S(1)}, u32[]{:S(2)}, u32[]{:S(2)}) %collective-permute-start.5) | collective-permute-done | bytes 393248 | tf_op jit(solution)/shard_map/ppermute | solution.py:35
  53.4 8.6 %collective-permute-done.6.refs_3_ = bf16[48,4096]{1,0:T(8,128)(2,1)S(1)} collective-permute-done((bf16[48,4096]{1,0:T(8,128)(2,1)S(1)}, bf16[48,4096]{1,0:T(8,128)(2,1)S(1)}, u32[]{:S(2)}, u32[]{:S(2)}) %collective-permute-start.6) | collective-permute-done | bytes 393248 | tf_op jit(solution)/shard_map/ppermute | solution.py:35
  62.0 2.8 %shard_map.78 = (bf16[48,4096]{1,0:T(8,128)(2,1)S(1)}, bf16[48,4096]{1,0:T(8,128)(2,1)S(1)}, bf16[48,4096]{1,0:T(8,128)(2,1)S(1)}, bf16[48,4096]{1,0:T(8,128)(2,...) custom-call(bf16[128,4224]{1,0:T(8,128)(2,1)S(1)} %collective-permute-done.1.refs_0_.refs_2_, ...), custom_call_target="tpu_custom_call" | custom-call | flops 131072 | bytes 3072 | tf_op jit(solution)/shard_map/pallas_call | solution.py:143
  64.8 3.3 %collective-permute-start.14 = (bf16[48,4096]{1,0:T(8,128)(2,1)S(1)}, bf16[48,4096]{1,0:T(8,128)(2,1)S(1)}, u32[]{:S(2)}, u32[]{:S(2)}) collective-permute-start(bf16[48,4096]{1,0:T(8,128)(2,1)S(1)} %get-tuple-element.85), channel_id=1, source_target_pairs={{0,2},{1,3},{2,0},{3,1},{4,6},{5,7},{6,4},{7,5},{8,10},{9,11},{10,... | collective-permute-start | bytes 1179656 | tf_op jit(solution)/shard_map/ppermute | solution.py:35
  68.1 2.3 %collective-permute-start.15 = (bf16[48,4096]{1,0:T(8,128)(2,1)S(1)}, bf16[48,4096]{1,0:T(8,128)(2,1)S(1)}, u32[]{:S(2)}, u32[]{:S(2)}) collective-permute-start(bf16[48,4096]{1,0:T(8,128)(2,1)S(1)} %get-tuple-element.86), channel_id=1, source_target_pairs={{0,3},{1,2},{2,1},{3,0},{4,7},{5,6},{6,5},{7,4},{8,11},{9,10},{10,... | collective-permute-start | bytes 1179656 | tf_op jit(solution)/shard_map/ppermute | solution.py:35
  70.4 2.7 %collective-permute-start.8 = (bf16[64,4096]{1,0:T(8,128)(2,1)S(1)}, bf16[64,4096]{1,0:T(8,128)(2,1)S(1)}, u32[]{:S(2)}, u32[]{:S(2)}) collective-permute-start(bf16[64,4096]{1,0:T(8,128)(2,1)S(1)} %get-tuple-element.73), channel_id=1, source_target_pairs={{0,28},{1,29},{2,30},{3,31},{4,0},{5,1},{6,2},{7,3},{8,4},{9,5},{1... | collective-permute-start | bytes 1572872 | tf_op jit(solution)/shard_map/ppermute | solution.py:31
  73.7 8.5 %shard_map.79 = (bf16[512,4096]{1,0:T(8,128)(2,1)S(1)}, bf16[512,2304]{1,0:T(8,128)(2,1)S(1)}, bf16[512,2176]{1,0:T(8,128)(2,1)S(1)}) custom-call(bf16[2048,2304]{1,0:T(8,128)(2,1)S(1)} %bitcast.7, bf16[2048,2304]{1,0:T(8,128)(2,1)S(1)} %bitcast.8, bf16[2048,2304]{1,0:T(8,128)(2,1)S(1)} %bitcast.9, bf16[48,4096]{1,0:T(8,128)(2,1)S(1)} %get-tuple-element.74.refs_0_, ...), custom_call_target="tpu_custom_call" | custom-call | flops 2949120 | bytes 9216 | tf_op jit(solution)/shard_map/pallas_call | solution.py:259
  82.2 3.7 %collective-permute-done.15.refs_3_ = bf16[48,4096]{1,0:T(8,128)(2,1)S(1)} collective-permute-done((bf16[48,4096]{1,0:T(8,128)(2,1)S(1)}, bf16[48,4096]{1,0:T(8,128)(2,1)S(1)}, u32[]{:S(2)}, u32[]{:S(2)}) %collective-permute-start.15) | collective-permute-done | bytes 393248 | tf_op jit(solution)/shard_map/ppermute | solution.py:35
  92.6 6.6 %shard_map.80 = (bf16[512,4096]{1,0:T(8,128)(2,1)S(1)}, bf16[512,2304]{1,0:T(8,128)(2,1)S(1)}, bf16[512,2176]{1,0:T(8,128)(2,1)S(1)}) custom-call(bf16[2048,2304]{1,0:T(8,128)(2,1)S(1)} %bitcast.10, bf16[2048,2304]{1,0:T(8,128)(2,1)S(1)} %bitcast.11, bf16[2048,2304]{1,0:T(8,128)(2,1)S(1)} %bitcast.12, ...), custom_call_target="tpu_custom_call", output_to_operand_aliasing={{0}: (7, {}), {1}: (8, {}), {2}: (9, {})} | custom-call | flops 1966080 | bytes 9216 | tf_op jit(solution)/shard_map/pallas_call | solution.py:259
  99.3 5.1 %collective-permute-done.10.refs_2_ = bf16[32,4096]{1,0:T(8,128)(2,1)S(1)} collective-permute-done((bf16[32,4096]{1,0:T(8,128)(2,1)S(1)}, bf16[32,4096]{1,0:T(8,128)(2,1)S(1)}, u32[]{:S(2)}, u32[]{:S(2)}) %collective-permute-start.10) | collective-permute-done | bytes 262176 | tf_op jit(solution)/shard_map/ppermute | solution.py:35
  104.4 3.8 %shard_map.81 = (bf16[512,4096]{1,0:T(8,128)(2,1)S(1)}, bf16[512,2304]{1,0:T(8,128)(2,1)S(1)}, f32[192,128]{1,0:T(8,128)S(1)}) custom-call(bf16[2048,2304]{1,0:T(8,128)(2,1)S(1)} %bitcast.13, bf16[2048,2304]{1,0:T(8,128)(2,1)S(1)} %bitcast.14, bf16[2048,2304]{1,0:T(8,128)(2,1)S(1)} %bitcast.15, ...), custom_call_target="tpu_custom_call", output_to_operand_aliasing={{0}: (9, {}), {1}: (10, {})} | custom-call | flops 1769472 | bytes 9216 | tf_op jit(solution)/shard_map/pallas_call | solution.py:259
  111.6 4.6 %shard_map.83 = (bf16[256,3840]{1,0:T(8,128)(2,1)}, bf16[256,3840]{1,0:T(8,128)(2,1)}) custom-call(bf16[512,4096]{1,0:T(8,128)(2,1)S(1)} %get-tuple-element.96.refs_0_.refs_1_, bf16[512,4096]{1,0:T(8,128)(2,1)S(1)} %get-tuple-element.96.refs_0_.refs_1_, bf16[512,2304]{1,0:T(8,128)(2,1)S(1)} %get-tuple-element.111.refs_2_.gate_f.up_f), custom_call_target="tpu_custom_call" | custom-call | flops 1966080 | bytes 3840 | tf_op jit(solution)/shard_map/pallas_call | solution.py:352
  116.2 2.7 %collective-permute-start.18 = (bf16[256,3840]{1,0:T(8,128)(2,1)}, bf16[256,3840]{1,0:T(8,128)(2,1)}, u32[]{:S(2)}, u32[]{:S(2)}) collective-permute-start(bf16[256,3840]{1,0:T(8,128)(2,1)} %get-tuple-element.103), channel_id=1, source_target_pairs={{0,192},{32,224},{64,0},{96,32},{128,64},{160,96},{192,128},{224,1... | collective-permute-start | bytes 5898248 | tf_op jit(solution)/shard_map/ppermute | solution.py:39
  120.2 4.5 %shard_map.87 = bf16[512,2176]{1,0:T(8,128)(2,1)S(1)} custom-call(bf16[2048,2304]{1,0:T(8,128)(2,1)S(1)} %bitcast.16, bf16[2048,2304]{1,0:T(8,128)(2,1)S(1)} %bitcast.17, bf16[512,2304]{1,0:T(8,128)(2,1)S(1)} %get-tuple-element.111.refs_2_.gate_f.up_f, bf16[512,2304]{1,0:T(8,128)(2,1)S(1)} %get-tuple-element.111.refs_2_.gate_f.up_f, ...), custom_call_target="tpu_custom_call", output_to_operand_aliasing={{}: (5, {})} | custom-call | flops 1179648 | bytes 6144 | tf_op jit(solution)/shard_map/pallas_call | solution.py:297
  126.2 11.1 %all-to-all-start = ((bf16[32,16,2176]{2,1,0:T(8,128)(2,1)}), bf16[32,16,2176]{2,1,0:T(8,128)(2,1)}, u32[]{:S(2)}, u32[]{:S(2)}) async-start(bf16[32,16,2176]{2,1,0:T(8,128)(2,1)} %bitcast.18), calls=%async_computation | async-start | bytes 4456448 | tf_op jit(solution)/shard_map/all_to_all | solution.py:510
  137.2 2.2 %copy-done.2 = bf16[512,4096]{1,0:T(8,128)(2,1)S(1)} copy-done((bf16[512,4096]{1,0:T(8,128)(2,1)S(1)}, bf16[512,4096]{1,0:T(8,128)(2,1)}, u32[]{:S(2)}) %copy-start.2) | copy-done | bytes 4194328
  142.8 19.8 %collective-permute-done.17.refs_3_.refs_1_ = bf16[256,3840]{1,0:T(8,128)(2,1)} collective-permute-done((bf16[256,3840]{1,0:T(8,128)(2,1)}, bf16[256,3840]{1,0:T(8,128)(2,1)}, u32[]{:S(2)}, u32[]{:S(2)}) %collective-permute-start.17) | collective-permute-done | bytes 1966112 | tf_op jit(solution)/shard_map/ppermute | solution.py:39
  165.2 2.0 collective-permute-start.25
  172.1 2.3 %shard_map.84 = (bf16[256,2304]{1,0:T(8,128)(2,1)S(1)}, bf16[256,2304]{1,0:T(8,128)(2,1)S(1)}) custom-call(bf16[512,4096]{1,0:T(8,128)(2,1)S(1)} %copy-done.2, bf16[512,4096]{1,0:T(8,128)(2,1)S(1)} %copy-done.2, bf16[512,2304]{1,0:T(8,128)(2,1)S(1)} %get-tuple-element.111.refs_2_.gate_f.up_f), custom_call_target="tpu_custom_call" | custom-call | flops 1179648 | bytes 2304 | tf_op jit(solution)/shard_map/pallas_call | solution.py:352
  175.7 3.7 %collective-permute-done.24.refs_2_ = bf16[256,768]{1,0:T(8,128)(2,1)S(1)} collective-permute-done((bf16[256,768]{1,0:T(8,128)(2,1)S(1)}, bf16[256,768]{1,0:T(8,128)(2,1)S(1)}, u32[]{:S(2)}, u32[]{:S(2)}) %collective-permute-start.24) | collective-permute-done | bytes 393248 | tf_op jit(solution)/shard_map/ppermute | solution.py:39
  180.8 7.0 %collective-permute-done.19.refs_2_ = bf16[256,768]{1,0:T(8,128)(2,1)S(1)} collective-permute-done((bf16[256,768]{1,0:T(8,128)(2,1)S(1)}, bf16[256,768]{1,0:T(8,128)(2,1)S(1)}, u32[]{:S(2)}, u32[]{:S(2)}) %collective-permute-start.19) | collective-permute-done | bytes 393248 | tf_op jit(solution)/shard_map/ppermute | solution.py:39
  189.2 1.9 shard_map.93.refs_4_
  191.2 4.8 %collective-permute-done.26.refs_3_ = bf16[256,768]{1,0:T(8,128)(2,1)S(1)} collective-permute-done((bf16[256,768]{1,0:T(8,128)(2,1)S(1)}, bf16[256,768]{1,0:T(8,128)(2,1)S(1)}, u32[]{:S(2)}, u32[]{:S(2)}) %collective-permute-start.26) | collective-permute-done | bytes 393248 | tf_op jit(solution)/shard_map/ppermute | solution.py:43
  196.0 1.9 shard_map.94.refs_4_
  197.9 3.2 %shard_map.88 = (bf16[128,2048]{1,0:T(8,128)(2,1)}, f32[2,128]{1,0:T(2,128)}) custom-call(s32[2,128]{1,0:T(2,128)S(1)} %bitcast.20, bf16[2,128]{1,0:T(2,128)(2,1)S(1)} %bitcast.22, bf16[512,2176]{1,0:T(8,128)(2,1)} %bitcast.4.back), custom_call_target="tpu_custom_call" | custom-call | flops 262144 | bytes 2048 | tf_op jit(solution)/shard_map/pallas_call | solution.py:448
  201.1 3.2 %collective-permute-done.21.refs_3_ = bf16[256,768]{1,0:T(8,128)(2,1)S(1)} collective-permute-done((bf16[256,768]{1,0:T(8,128)(2,1)S(1)}, bf16[256,768]{1,0:T(8,128)(2,1)S(1)}, u32[]{:S(2)}, u32[]{:S(2)}) %collective-permute-start.21) | collective-permute-done | bytes 393248 | tf_op jit(solution)/shard_map/ppermute | solution.py:43
  204.4 1.9 shard_map.95
  (85 shorter events, 34.3 us)
Async XLA Ops:
  4.5 29.0 %collective-permute-start.2 = (bf16[128,4224]{1,0:T(8,128)(2,1)S(1)}, bf16[128,4224]{1,0:T(8,128)(2,1)S(1)}, u32[]{:S(2)}, u32[]{:S(2)}) collective-permute-start(bf16[128,4224]{1,0:T(8,128)(2,1)S(1)} %shard_map.76.refs_0_.refs_3_), channel_id=1, source_target_pairs={{0,28},{1,29},{2,30},{3,31},{4,0},{5,1},{6,2},{7,3},{8,4},{9,5},{1... | collective-permute-start | bytes 3244040 | tf_op jit(solution)/shard_map/ppermute | solution.py:31
  10.9 25.9 %collective-permute-start = (bf16[128,4224]{1,0:T(8,128)(2,1)S(1)}, bf16[128,4224]{1,0:T(8,128)(2,1)S(1)}, u32[]{:S(2)}, u32[]{:S(2)}) collective-permute-start(bf16[128,4224]{1,0:T(8,128)(2,1)S(1)} %shard_map.76.refs_0_.refs_3_), channel_id=1, source_target_pairs={{0,4},{1,5},{2,6},{3,7},{4,8},{5,9},{6,10},{7,11},{8,12},{9,13},{1... | collective-permute-start | bytes 3244040 | tf_op jit(solution)/shard_map/ppermute | solution.py:31
  33.5 28.5 %collective-permute-start.3 = (bf16[128,4224]{1,0:T(8,128)(2,1)S(1)}, bf16[128,4224]{1,0:T(8,128)(2,1)S(1)}, u32[]{:S(2)}, u32[]{:S(2)}) collective-permute-start(bf16[128,4224]{1,0:T(8,128)(2,1)S(1)} %collective-permute-done.2.refs_2_.refs_5_), channel_id=1, source_target_pairs={{0,28},{1,29},{2,30},{3,31},{4,0},{5,1},{6,2},{7,3},{8,4},{9,5},{1... | collective-permute-start | bytes 3244040 | tf_op jit(solution)/shard_map/ppermute | solution.py:31
  36.9 25.1 %collective-permute-start.1 = (bf16[128,4224]{1,0:T(8,128)(2,1)S(1)}, bf16[128,4224]{1,0:T(8,128)(2,1)S(1)}, u32[]{:S(2)}, u32[]{:S(2)}) collective-permute-start(bf16[128,4224]{1,0:T(8,128)(2,1)S(1)} %collective-permute-done.refs_1_.refs_4_), channel_id=1, source_target_pairs={{0,4},{1,5},{2,6},{3,7},{4,8},{5,9},{6,10},{7,11},{8,12},{9,13},{1... | collective-permute-start | bytes 3244040 | tf_op jit(solution)/shard_map/ppermute | solution.py:31
  36.9 36.8 %copy-start = (bf16[1,2048,2304]{2,1,0:T(8,128)(2,1)S(1)}, bf16[1,2048,2304]{2,1,0:T(8,128)(2,1)}, u32[]{:S(2)}) copy-start(bf16[1,2048,2304]{2,1,0:T(8,128)(2,1)} %param.9) | copy-start | bytes 28311556
  39.3 5.2 %collective-permute-start.4 = (bf16[48,4096]{1,0:T(8,128)(2,1)S(1)}, bf16[48,4096]{1,0:T(8,128)(2,1)S(1)}, u32[]{:S(2)}, u32[]{:S(2)}) collective-permute-start(bf16[48,4096]{1,0:T(8,128)(2,1)S(1)} %get-tuple-element.68), channel_id=1, source_target_pairs={{0,1},{1,0},{2,3},{3,2},{4,5},{5,4},{6,7},{7,6},{8,9},{9,8},{10,11... | collective-permute-start | bytes 1179656 | tf_op jit(solution)/shard_map/ppermute | solution.py:35
  41.2 12.2 %collective-permute-start.5 = (bf16[48,4096]{1,0:T(8,128)(2,1)S(1)}, bf16[48,4096]{1,0:T(8,128)(2,1)S(1)}, u32[]{:S(2)}, u32[]{:S(2)}) collective-permute-start(bf16[48,4096]{1,0:T(8,128)(2,1)S(1)} %get-tuple-element.69), channel_id=1, source_target_pairs={{0,2},{1,3},{2,0},{3,1},{4,6},{5,7},{6,4},{7,5},{8,10},{9,11},{10,... | collective-permute-start | bytes 1179656 | tf_op jit(solution)/shard_map/ppermute | solution.py:35
  44.1 17.9 %collective-permute-start.6 = (bf16[48,4096]{1,0:T(8,128)(2,1)S(1)}, bf16[48,4096]{1,0:T(8,128)(2,1)S(1)}, u32[]{:S(2)}, u32[]{:S(2)}) collective-permute-start(bf16[48,4096]{1,0:T(8,128)(2,1)S(1)} %get-tuple-element.70), channel_id=1, source_target_pairs={{0,3},{1,2},{2,1},{3,0},{4,7},{5,6},{6,5},{7,4},{8,11},{9,10},{10,... | collective-permute-start | bytes 1179656 | tf_op jit(solution)/shard_map/ppermute | solution.py:35
  64.8 17.4 %collective-permute-start.14 = (bf16[48,4096]{1,0:T(8,128)(2,1)S(1)}, bf16[48,4096]{1,0:T(8,128)(2,1)S(1)}, u32[]{:S(2)}, u32[]{:S(2)}) collective-permute-start(bf16[48,4096]{1,0:T(8,128)(2,1)S(1)} %get-tuple-element.85), channel_id=1, source_target_pairs={{0,2},{1,3},{2,0},{3,1},{4,6},{5,7},{6,4},{7,5},{8,10},{9,11},{10,... | collective-permute-start | bytes 1179656 | tf_op jit(solution)/shard_map/ppermute | solution.py:35
  68.1 17.8 %collective-permute-start.15 = (bf16[48,4096]{1,0:T(8,128)(2,1)S(1)}, bf16[48,4096]{1,0:T(8,128)(2,1)S(1)}, u32[]{:S(2)}, u32[]{:S(2)}) collective-permute-start(bf16[48,4096]{1,0:T(8,128)(2,1)S(1)} %get-tuple-element.86), channel_id=1, source_target_pairs={{0,3},{1,2},{2,1},{3,0},{4,7},{5,6},{6,5},{7,4},{8,11},{9,10},{10,... | collective-permute-start | bytes 1179656 | tf_op jit(solution)/shard_map/ppermute | solution.py:35
  70.4 18.1 %collective-permute-start.7 = (bf16[64,4096]{1,0:T(8,128)(2,1)S(1)}, bf16[64,4096]{1,0:T(8,128)(2,1)S(1)}, u32[]{:S(2)}, u32[]{:S(2)}) collective-permute-start(bf16[64,4096]{1,0:T(8,128)(2,1)S(1)} %get-tuple-element.72), channel_id=1, source_target_pairs={{0,4},{1,5},{2,6},{3,7},{4,8},{5,9},{6,10},{7,11},{8,12},{9,13},{1... | collective-permute-start | bytes 1572872 | tf_op jit(solution)/shard_map/ppermute | solution.py:31
  70.4 18.1 %collective-permute-start.8 = (bf16[64,4096]{1,0:T(8,128)(2,1)S(1)}, bf16[64,4096]{1,0:T(8,128)(2,1)S(1)}, u32[]{:S(2)}, u32[]{:S(2)}) collective-permute-start(bf16[64,4096]{1,0:T(8,128)(2,1)S(1)} %get-tuple-element.73), channel_id=1, source_target_pairs={{0,28},{1,29},{2,30},{3,31},{4,0},{5,1},{6,2},{7,3},{8,4},{9,5},{1... | collective-permute-start | bytes 1572872 | tf_op jit(solution)/shard_map/ppermute | solution.py:31
  73.1 13.9 %collective-permute-start.12 = (bf16[48,4096]{1,0:T(8,128)(2,1)S(1)}, bf16[48,4096]{1,0:T(8,128)(2,1)S(1)}, u32[]{:S(2)}, u32[]{:S(2)}) collective-permute-start(bf16[48,4096]{1,0:T(8,128)(2,1)S(1)} %get-tuple-element.84), channel_id=1, source_target_pairs={{0,1},{1,0},{2,3},{3,2},{4,5},{5,4},{6,7},{7,6},{8,9},{9,8},{10,11... | collective-permute-start | bytes 1179656 | tf_op jit(solution)/shard_map/ppermute | solution.py:35
  86.0 13.3 %collective-permute-start.16 = (bf16[32,4096]{1,0:T(8,128)(2,1)S(1)}, bf16[32,4096]{1,0:T(8,128)(2,1)S(1)}, u32[]{:S(2)}, u32[]{:S(2)}) collective-permute-start(bf16[32,4096]{1,0:T(8,128)(2,1)S(1)} %pad_maximum_fusion.5), channel_id=1, source_target_pairs={{0,24},{1,25},{2,26},{3,27},{4,28},{5,29},{6,30},{7,31},{8,0},{9,1... | collective-permute-start | bytes 786440 | tf_op jit(solution)/shard_map/ppermute | solution.py:31
  87.0 12.3 %collective-permute-start.13 = (bf16[32,4096]{1,0:T(8,128)(2,1)S(1)}, bf16[32,4096]{1,0:T(8,128)(2,1)S(1)}, u32[]{:S(2)}, u32[]{:S(2)}) collective-permute-start(bf16[32,4096]{1,0:T(8,128)(2,1)S(1)} %pad_maximum_fusion.4), channel_id=1, source_target_pairs={{0,8},{1,9},{2,10},{3,11},{4,12},{5,13},{6,14},{7,15},{8,16},{9,17... | collective-permute-start | bytes 786440 | tf_op jit(solution)/shard_map/ppermute | solution.py:31
  88.7 10.7 %collective-permute-start.11 = (bf16[32,4096]{1,0:T(8,128)(2,1)S(1)}, bf16[32,4096]{1,0:T(8,128)(2,1)S(1)}, u32[]{:S(2)}, u32[]{:S(2)}) collective-permute-start(bf16[32,4096]{1,0:T(8,128)(2,1)S(1)} %pad_maximum_fusion.3), channel_id=1, source_target_pairs={{0,3},{1,2},{2,1},{3,0},{4,7},{5,6},{6,5},{7,4},{8,11},{9,10},{10,... | collective-permute-start | bytes 786440 | tf_op jit(solution)/shard_map/ppermute | solution.py:35
  90.5 13.9 %collective-permute-start.10 = (bf16[32,4096]{1,0:T(8,128)(2,1)S(1)}, bf16[32,4096]{1,0:T(8,128)(2,1)S(1)}, u32[]{:S(2)}, u32[]{:S(2)}) collective-permute-start(bf16[32,4096]{1,0:T(8,128)(2,1)S(1)} %pad_maximum_fusion.2), channel_id=1, source_target_pairs={{0,2},{1,3},{2,0},{3,1},{4,6},{5,7},{6,4},{7,5},{8,10},{9,11},{10,... | collective-permute-start | bytes 786440 | tf_op jit(solution)/shard_map/ppermute | solution.py:35
  92.2 12.2 %collective-permute-start.9 = (bf16[32,4096]{1,0:T(8,128)(2,1)S(1)}, bf16[32,4096]{1,0:T(8,128)(2,1)S(1)}, u32[]{:S(2)}, u32[]{:S(2)}) collective-permute-start(bf16[32,4096]{1,0:T(8,128)(2,1)S(1)} %pad_maximum_fusion.1), channel_id=1, source_target_pairs={{0,1},{1,0},{2,3},{3,2},{4,5},{5,4},{6,7},{7,6},{8,9},{9,8},{10,11... | collective-permute-start | bytes 786440 | tf_op jit(solution)/shard_map/ppermute | solution.py:35
  108.9 11.4 %collective-permute-start.22 = (bf16[256,768]{1,0:T(8,128)(2,1)S(1)}, bf16[256,768]{1,0:T(8,128)(2,1)S(1)}, u32[]{:S(2)}, u32[]{:S(2)}) collective-permute-start(bf16[256,768]{1,0:T(8,128)(2,1)S(1)} %get-tuple-element.109), channel_id=1, source_target_pairs={{0,64},{32,96},{64,128},{96,160},{128,192},{160,224},{192,0},{224,... | collective-permute-start | bytes 1179656 | tf_op jit(solution)/shard_map/ppermute | solution.py:39
  110.0 10.2 %collective-permute-start.23 = (bf16[256,768]{1,0:T(8,128)(2,1)S(1)}, bf16[256,768]{1,0:T(8,128)(2,1)S(1)}, u32[]{:S(2)}, u32[]{:S(2)}) collective-permute-start(bf16[256,768]{1,0:T(8,128)(2,1)S(1)} %get-tuple-element.110), channel_id=1, source_target_pairs={{0,192},{32,224},{64,0},{96,32},{128,64},{160,96},{192,128},{224,1... | collective-permute-start | bytes 1179656 | tf_op jit(solution)/shard_map/ppermute | solution.py:39
  116.2 46.4 %collective-permute-start.17 = (bf16[256,3840]{1,0:T(8,128)(2,1)}, bf16[256,3840]{1,0:T(8,128)(2,1)}, u32[]{:S(2)}, u32[]{:S(2)}) collective-permute-start(bf16[256,3840]{1,0:T(8,128)(2,1)} %get-tuple-element.102), channel_id=1, source_target_pairs={{0,64},{32,96},{64,128},{96,160},{128,192},{160,224},{192,0},{224,... | collective-permute-start | bytes 5898248 | tf_op jit(solution)/shard_map/ppermute | solution.py:39
  116.2 46.4 %collective-permute-start.18 = (bf16[256,3840]{1,0:T(8,128)(2,1)}, bf16[256,3840]{1,0:T(8,128)(2,1)}, u32[]{:S(2)}, u32[]{:S(2)}) collective-permute-start(bf16[256,3840]{1,0:T(8,128)(2,1)} %get-tuple-element.103), channel_id=1, source_target_pairs={{0,192},{32,224},{64,0},{96,32},{128,64},{160,96},{192,128},{224,1... | collective-permute-start | bytes 5898248 | tf_op jit(solution)/shard_map/ppermute | solution.py:39
  126.2 71.7 %all-to-all-start = ((bf16[32,16,2176]{2,1,0:T(8,128)(2,1)}), bf16[32,16,2176]{2,1,0:T(8,128)(2,1)}, u32[]{:S(2)}, u32[]{:S(2)}) async-start(bf16[32,16,2176]{2,1,0:T(8,128)(2,1)} %bitcast.18), calls=%async_computation | async-start | bytes 4456448 | tf_op jit(solution)/shard_map/all_to_all | solution.py:510
  140.0 30.9 %collective-permute-start.27 = (bf16[256,768]{1,0:T(8,128)(2,1)S(1)}, bf16[256,768]{1,0:T(8,128)(2,1)S(1)}, u32[]{:S(2)}, u32[]{:S(2)}) collective-permute-start(bf16[256,768]{1,0:T(8,128)(2,1)S(1)} %get-tuple-element.127), channel_id=1, source_target_pairs={{0,64},{32,96},{64,128},{96,160},{128,192},{160,224},{192,0},{224,... | collective-permute-start | bytes 1179656 | tf_op jit(solution)/shard_map/ppermute | solution.py:39
  141.3 33.1 %collective-permute-start.28 = (bf16[256,768]{1,0:T(8,128)(2,1)S(1)}, bf16[256,768]{1,0:T(8,128)(2,1)S(1)}, u32[]{:S(2)}, u32[]{:S(2)}) collective-permute-start(bf16[256,768]{1,0:T(8,128)(2,1)S(1)} %get-tuple-element.128), channel_id=1, source_target_pairs={{0,192},{32,224},{64,0},{96,32},{128,64},{160,96},{192,128},{224,1... | collective-permute-start | bytes 1179656 | tf_op jit(solution)/shard_map/ppermute | solution.py:39
  164.4 15.0 %collective-permute-start.24 = (bf16[256,768]{1,0:T(8,128)(2,1)S(1)}, bf16[256,768]{1,0:T(8,128)(2,1)S(1)}, u32[]{:S(2)}, u32[]{:S(2)}) collective-permute-start(bf16[256,768]{1,0:T(8,128)(2,1)S(1)} %get-tuple-element.121), channel_id=1, source_target_pairs={{0,64},{32,96},{64,128},{96,160},{128,192},{160,224},{192,0},{224,... | collective-permute-start | bytes 1179656 | tf_op jit(solution)/shard_map/ppermute | solution.py:39
  165.2 14.3 %collective-permute-start.25 = (bf16[256,768]{1,0:T(8,128)(2,1)S(1)}, bf16[256,768]{1,0:T(8,128)(2,1)S(1)}, u32[]{:S(2)}, u32[]{:S(2)}) collective-permute-start(bf16[256,768]{1,0:T(8,128)(2,1)S(1)} %get-tuple-element.122), channel_id=1, source_target_pairs={{0,192},{32,224},{64,0},{96,32},{128,64},{160,96},{192,128},{224,1... | collective-permute-start | bytes 1179656 | tf_op jit(solution)/shard_map/ppermute | solution.py:39
  169.0 18.8 %collective-permute-start.19 = (bf16[256,768]{1,0:T(8,128)(2,1)S(1)}, bf16[256,768]{1,0:T(8,128)(2,1)S(1)}, u32[]{:S(2)}, u32[]{:S(2)}) collective-permute-start(bf16[256,768]{1,0:T(8,128)(2,1)S(1)} %get-tuple-element.106), channel_id=1, source_target_pairs={{0,64},{32,96},{64,128},{96,160},{128,192},{160,224},{192,0},{224,... | collective-permute-start | bytes 1179656 | tf_op jit(solution)/shard_map/ppermute | solution.py:39
  170.9 16.9 %collective-permute-start.20 = (bf16[256,768]{1,0:T(8,128)(2,1)S(1)}, bf16[256,768]{1,0:T(8,128)(2,1)S(1)}, u32[]{:S(2)}, u32[]{:S(2)}) collective-permute-start(bf16[256,768]{1,0:T(8,128)(2,1)S(1)} %get-tuple-element.107), channel_id=1, source_target_pairs={{0,192},{32,224},{64,0},{96,32},{128,64},{160,96},{192,128},{224,1... | collective-permute-start | bytes 1179656 | tf_op jit(solution)/shard_map/ppermute | solution.py:39
  175.6 13.6 %collective-permute-start.29 = (bf16[256,768]{1,0:T(8,128)(2,1)S(1)}, bf16[256,768]{1,0:T(8,128)(2,1)S(1)}, u32[]{:S(2)}, u32[]{:S(2)}) collective-permute-start(bf16[256,768]{1,0:T(8,128)(2,1)S(1)} %shard_map.92), channel_id=1, source_target_pairs={{0,32},{32,0},{64,96},{96,64},{128,160},{160,128},{192,224},{224,1... | collective-permute-start | bytes 1179656 | tf_op jit(solution)/shard_map/ppermute | solution.py:43
  180.7 15.3 %collective-permute-start.26 = (bf16[256,768]{1,0:T(8,128)(2,1)S(1)}, bf16[256,768]{1,0:T(8,128)(2,1)S(1)}, u32[]{:S(2)}, u32[]{:S(2)}) collective-permute-start(bf16[256,768]{1,0:T(8,128)(2,1)S(1)} %shard_map.90), channel_id=1, source_target_pairs={{0,32},{32,0},{64,96},{96,64},{128,160},{160,128},{192,224},{224,1... | collective-permute-start | bytes 1179656 | tf_op jit(solution)/shard_map/ppermute | solution.py:43
  189.1 15.3 %collective-permute-start.21 = (bf16[256,768]{1,0:T(8,128)(2,1)S(1)}, bf16[256,768]{1,0:T(8,128)(2,1)S(1)}, u32[]{:S(2)}, u32[]{:S(2)}) collective-permute-start(bf16[256,768]{1,0:T(8,128)(2,1)S(1)} %shard_map.86), channel_id=1, source_target_pairs={{0,32},{32,0},{64,96},{96,64},{128,160},{160,128},{192,224},{224,1... | collective-permute-start | bytes 1179656 | tf_op jit(solution)/shard_map/ppermute | solution.py:43
  (11 other events, 33.7 us)
